TPU v7x, 32 devices: a whole 2x2x4 slice. The times are simulated.
32 devices in a mesh: rep: 16 (over z, y, core), seq: 2 (over x).
Axes of the slice: x: 2, y: 2, z: 4, core: 2. Of those that a mesh axis runs over, the one named last changes fastest.
Arguments:
- text_tokens: bfloat16 [16, 512, 3072], P('rep', 'seq'), may hold values from -6 to 6
- image_tokens: bfloat16 [16, 576, 3072], P('rep', 'seq'), may hold values from -6 to 6
- weights: bfloat16 [2, 3072, 3, 3072], P(None, ('rep', 'seq'))
- qk_gain: float32 [2, 2, 128], replicated, may hold values from 0.5 to 4.2, as said below
- mod_table: float32 [28, 2, 2, 3072], replicated, may hold values from -3 to 3
- text_lengths: int32 [16], P('rep'), may hold values from 64 to 512, as said below
- time_index: int32 [16], P('rep'), may hold values from 0 to 27
Outputs:
- attended_text: bfloat16 [16, 512, 3072], P('rep', 'seq')
- attended_image: bfloat16 [16, 576, 3072], P('rep', 'seq')
Inputs may be any that keep to these rules, and one draw needn't show every extreme that they name: `text_lengths`: padding of a prompt lies past its length; some prompt fills all 512 text tokens. `qk_gain`: positive gains.
All inputs are finite; a program needn't handle non-finite values.
Results may differ from a plain program's by a relative error of at most 0.01.
Values may be sent and summed in bfloat16 or wider, within the bound.
No kernel may reach another device: no remote copies, remote signals or barrier semaphores. Data moves between devices by JAX's collectives and lax.ppermute only.
A program may use at most 192 MiB of HBM per device.

v0:
```python
import jax
import jax.numpy as jnp
from jax import lax
from jax.sharding import PartitionSpec as P

D = 3072
HD = 128
GRID = 24
TXT = 512


def layer_modulate(tokens, shift_row, scale_row):
    values = tokens.astype(jnp.float32)
    center = values - jnp.mean(values, axis=-1, keepdims=True)
    spread = jnp.mean(center * center, axis=-1, keepdims=True)
    normed = center * lax.rsqrt(spread + 1e-06)
    return (normed * (1.0 + shift_row * 0.0 + scale_row) + shift_row).astype(jnp.bfloat16)


def rope_tables(length, text_count, grid_side, head_dim):
    pair_count = head_dim // 2
    still_pairs = head_dim // 16
    row_pairs = (pair_count - still_pairs) // 2
    col_pairs = pair_count - still_pairs - row_pairs
    position = jnp.arange(length, dtype=jnp.int32)
    image_pos = jnp.maximum(position - text_count, 0)
    is_image = (position >= text_count).astype(jnp.float32)
    row_pos = (image_pos // grid_side).astype(jnp.float32) * is_image
    col_pos = (image_pos % grid_side).astype(jnp.float32) * is_image
    row_freq = 10000.0 ** (-jnp.arange(row_pairs, dtype=jnp.float32) / row_pairs)
    col_freq = 10000.0 ** (-jnp.arange(col_pairs, dtype=jnp.float32) / col_pairs)
    angles = jnp.concatenate(
        [
            jnp.zeros((length, still_pairs), jnp.float32),
            row_pos[:, None] * row_freq[None, :],
            col_pos[:, None] * col_freq[None, :],
        ],
        axis=1,
    )
    return (jnp.cos(angles), jnp.sin(angles))


def rotate(values, cosine, sine):
    shaped = values.reshape(values.shape[0], values.shape[1], -1, 2)
    first_part = shaped[..., 0]
    second_part = shaped[..., 1]
    cos_part = cosine[:, None, :]
    sin_part = sine[:, None, :]
    turned = jnp.stack(
        [
            first_part * cos_part - second_part * sin_part,
            first_part * sin_part + second_part * cos_part,
        ],
        axis=-1,
    )
    return turned.reshape(values.shape)


def normalize_heads(values, gain):
    power = jnp.mean(values * values, axis=-1, keepdims=True)
    return values * lax.rsqrt(power + 1e-06) * gain


def prepare_heads(projected, gain, cosine, sine):
    query = rotate(normalize_heads(projected[:, 0], gain[0]), cosine, sine).astype(jnp.bfloat16)
    key_part = rotate(normalize_heads(projected[:, 1], gain[1]), cosine, sine).astype(jnp.bfloat16)
    value_part = projected[:, 2].astype(jnp.bfloat16)
    return (query, key_part, value_part)


def attend_head(query_head, key_head, value_head, allowed):
    scores = lax.dot_general(
        query_head, key_head, (((1,), (1,)), ((), ())), preferred_element_type=jnp.float32
    )
    scores = scores * query_head.shape[-1] ** (-0.5)
    scores = jnp.where(allowed[None, :], scores, -jnp.inf)
    row_max = jnp.max(scores, axis=-1, keepdims=True)
    exponent = jnp.exp(scores - row_max)
    softmax_out = (exponent / jnp.sum(exponent, axis=-1, keepdims=True)).astype(jnp.bfloat16)
    return jnp.dot(softmax_out, value_head, preferred_element_type=jnp.float32).astype(jnp.bfloat16)


def run_attention(queries, keys_all, values_all, allowed):

    def one_head(trio):
        return attend_head(trio[0], trio[1], trio[2], allowed)

    stacked = (
        jnp.moveaxis(queries, 1, 0),
        jnp.moveaxis(keys_all, 1, 0),
        jnp.moveaxis(values_all, 1, 0),
    )
    outputs = lax.map(one_head, stacked)
    outputs = jnp.moveaxis(outputs, 0, 1)
    return outputs.reshape(outputs.shape[0], -1)


def on_device(text_tokens, image_tokens, weights, qk_gain, mod_table, text_lengths, time_index):
    seq_count = lax.axis_size("seq")
    col_count = weights.shape[3] // seq_count
    heads_here = col_count // HD
    total_rows = TXT + GRID * GRID
    cosine_all, sine_all = rope_tables(total_rows, TXT, GRID, HD)
    picker = (jnp.arange(mod_table.shape[0], dtype=jnp.int32) == time_index[0]).astype(jnp.float32)
    table_row = jnp.sum(mod_table * picker[:, None, None, None], axis=0)
    prepared = []
    for stream in range(2):
        rows_here = (text_tokens, image_tokens)[stream][0]
        modded = layer_modulate(rows_here, table_row[stream, 0], table_row[stream, 1])
        relaid = lax.all_to_all(weights[stream], "seq", split_axis=2, concat_axis=0, tiled=True)
        full_weight = lax.all_gather(relaid, "rep", axis=0, tiled=True)
        all_rows = lax.all_gather(modded, "seq", axis=0, tiled=True)
        projected = jnp.dot(
            all_rows, full_weight.reshape(D, 3 * col_count), preferred_element_type=jnp.float32
        )
        row_count = projected.shape[0]
        offset_rows = 0 if stream == 0 else TXT
        projected = projected.reshape(row_count, 3, heads_here, HD)
        prepared.append(
            prepare_heads(
                projected,
                qk_gain[stream],
                cosine_all[offset_rows : offset_rows + row_count],
                sine_all[offset_rows : offset_rows + row_count],
            )
        )
    queries = jnp.concatenate([prepared[0][0], prepared[1][0]], axis=0)
    keys_all = jnp.concatenate([prepared[0][1], prepared[1][1]], axis=0)
    values_all = jnp.concatenate([prepared[0][2], prepared[1][2]], axis=0)
    position = jnp.arange(total_rows, dtype=jnp.int32)
    allowed = (position >= TXT) | (position < text_lengths[0])
    joined = run_attention(queries, keys_all, values_all, allowed)
    text_out, image_out = (
        lax.all_to_all(joined[:TXT], "seq", split_axis=0, concat_axis=1, tiled=True),
        lax.all_to_all(joined[TXT:], "seq", split_axis=0, concat_axis=1, tiled=True),
    )
    return (text_out[None], image_out[None])


def solution(mesh):
    placed = (
        P("rep", "seq", None),
        P("rep", "seq", None),
        P(None, ("rep", "seq"), None, None),
        P(),
        P(),
        P("rep"),
        P("rep"),
    )
    return jax.shard_map(
        on_device,
        mesh=mesh,
        in_specs=placed,
        out_specs=(P("rep", "seq", None), P("rep", "seq", None)),
        check_vma=False,
    )
```

profile of v0, /device:TPU:0, one launch (start us, length us, event | category | flops | bytes accessed | tf_op | source)
XLA Modules:
  0.0 728.1 jit_solution(3499300927342279503)
XLA Ops:
  7.2 4.3 fusion.49
  11.5 4.2 copy.57
  15.8 41.1 %all_to_all.68 = bf16[96,3,3072]{0,1,2:T(4,128)(2,1)} all-to-all(bf16[96,3,3072]{0,1,2:T(4,128)(2,1)S(1)} %bitcast.137), channel_id=1, replica_groups=mesh['rep'=16,'seq'=2] {'seq'}, dimensions={2} | all-to-all | bytes 3538944 | tf_op jit(solution)/shard_map/all_to_all | solution.py:110
  56.9 7.6 %copy.55 = bf16[96,3,2,1536]{3,2,0,1:T(2,128)(2,1)S(1)} copy(bf16[96,3,2,1536]{0,1,3,2:T(4,128)(2,1)} %bitcast.138) | data formatting | bytes 3538944 | tf_op jit(solution)/shard_map/all_to_all | solution.py:110
  65.9 4.2 copy.58
  70.2 39.4 %all_to_all.69 = bf16[96,3,3072]{0,1,2:T(4,128)(2,1)} all-to-all(bf16[96,3,3072]{0,1,2:T(4,128)(2,1)S(1)} %bitcast.139), channel_id=1, replica_groups=mesh['rep'=16,'seq'=2] {'seq'}, dimensions={2} | all-to-all | bytes 3538944 | tf_op jit(solution)/shard_map/all_to_all | solution.py:110
  109.6 7.6 %copy.56 = bf16[96,3,2,1536]{3,2,0,1:T(2,128)(2,1)S(1)} copy(bf16[96,3,2,1536]{0,1,3,2:T(4,128)(2,1)} %bitcast.140) | data formatting | bytes 3538944 | tf_op jit(solution)/shard_map/all_to_all | solution.py:110
  133.5 76.5 %all-gather.7.cloned.1.call-done = bf16[3072,3,1536]{2,0,1:T(8,128)(2,1)} async-done(((bf16[192,3,1536]{2,0,1:T(8,128)(2,1)}), bf16[3072,3,1536]{2,0,1:T(8,128)(2,1)}) %all-gather.7.cloned.1.call-update) | async-done | bytes 28311568 | tf_op jit(solution)/shard_map/all_gather | solution.py:111
  210.0 34.7 %copy.38 = bf16[3072,3,1536]{0,2,1:T(8,128)(2,1)} copy(bf16[3072,3,1536]{2,0,1:T(8,128)(2,1)} %all-gather.7.cloned.1.call-done) | data formatting | bytes 56623104 | tf_op jit(solution)/shard_map/all_gather | solution.py:111
  244.7 110.8 %all-gather.11.cloned.1.call-done = bf16[3072,3,1536]{2,0,1:T(8,128)(2,1)} async-done(((bf16[192,3,1536]{2,0,1:T(8,128)(2,1)}), bf16[3072,3,1536]{2,0,1:T(8,128)(2,1)}) %all-gather.11.cloned.1.call-update) | async-done | bytes 28311568 | tf_op jit(solution)/shard_map/all_gather | solution.py:111
  355.5 36.8 %copy.42 = bf16[3072,3,1536]{0,2,1:T(8,128)(2,1)} copy(bf16[3072,3,1536]{2,0,1:T(8,128)(2,1)} %all-gather.11.cloned.1.call-done) | data formatting | bytes 56623104 | tf_op jit(solution)/shard_map/all_gather | solution.py:111
  392.3 10.3 %all-gather.5.cloned.1.call-done = bf16[512,3072]{1,0:T(8,128)(2,1)} async-done(((bf16[256,3072]{1,0:T(8,128)(2,1)}), bf16[512,3072]{1,0:T(8,128)(2,1)}) %all-gather.5.cloned.1.call-update) | async-done | bytes 3145744 | tf_op jit(solution)/shard_map/all_gather | solution.py:112
  402.6 19.8 %fusion.33 = f32[512,3,12,128]{0,3,2,1:T(8,128)S(1)} fusion(bf16[3,12,128,3072]{3,2,1,0:T(8,128)(2,1)} %bitcast.136, bf16[512,3072]{1,0:T(8,128)(2,1)} %all-gather.5.cloned.1.call-done), kind=kOutput, calls=%fused_computation.50 | convolution fusion | flops 14495514624 | bytes 40894464 | tf_op jit(solution)/shard_map/dot_general | solution.py:113
  423.8 4.7 multiply_reduce_fusion.2
  428.5 24.9 %all-gather.9.cloned.1.call-done = bf16[576,3072]{1,0:T(8,128)(2,1)} async-done(((bf16[288,3072]{1,0:T(8,128)(2,1)}), bf16[576,3072]{1,0:T(8,128)(2,1)}) %all-gather.9.cloned.1.call-update) | async-done | bytes 3538960 | tf_op jit(solution)/shard_map/all_gather | solution.py:112
  453.4 23.1 %fusion.24 = f32[576,3,12,128]{3,0,2,1:T(8,128)S(1)} fusion(bf16[3,12,128,3072]{3,2,1,0:T(8,128)(2,1)} %bitcast.135, bf16[576,3072]{1,0:T(8,128)(2,1)} %all-gather.9.cloned.1.call-done), kind=kOutput, calls=%fused_computation.37 | convolution fusion | flops 16307453952 | bytes 42467328 | tf_op jit(solution)/shard_map/dot_general | solution.py:113
  478.1 4.4 multiply_reduce_fusion
  485.1 5.2 squeeze.70
  490.3 5.4 squeeze.65
  502.0 9.2 %subtract_convert_fusion.2 = (bf16[512,12,64,1]{0,3,2,1:T(2,128)(2,1)S(1)}, bf16[512,12,64,1]{0,3,2,1:T(2,128)(2,1)S(1)}, bf16[512,12,64,1]{0,3,2,1:T(2,128)(2,1)}, bf16[512,12,64,1]{0,3,2,1:T(2,128)(2,1)}) fusion(f32[512,12,64,2]{0,3,2,1:T(2,128)S(1)} %multiply_multiply_fusion.2, f32[512,64]{0,1:T(8,128)S(1)} %copy-done.10, f32[512,64]{0,1:T(8,128)S(1)} %copy-done.9, ...), kind=kLoop, calls=%fused_computation.67 | loop fusion | flops 6291456 | bytes 9699328 | tf_op jit(solution)/shard_map/convert.4
  519.0 5.6 pad_maximum_fusion.2
  528.2 5.3 copy.44
  533.4 5.6 squeeze.71
  542.2 5.8 squeeze.69
  548.1 4.2 multiply_multiply_fusion
  554.3 11.1 %subtract_convert_fusion = (bf16[576,12,64,1]{0,3,2,1:T(2,128)(2,1)S(1)}, bf16[576,12,64,1]{0,3,2,1:T(2,128)(2,1)S(1)}, bf16[576,12,64,1]{0,3,2,1:T(2,128)(2,1)}, bf16[576,12,64,1]{0,3,2,1:T(2,128)(2,1)}) fusion(f32[576,12,64,2]{0,3,2,1:T(2,128)S(1)} %multiply_multiply_fusion, f32[576,64]{0,1:T(8,128)S(1)} %copy-done.8, f32[576,64]{0,1:T(8,128)S(1)} %copy-done.7, ...), kind=kLoop, calls=%fused_computation.59 | loop fusion | flops 7077888 | bytes 10911744 | tf_op jit(solution)/shard_map/convert.2
  565.4 4.6 pad_maximum_fusion.1
  579.1 6.7 pad_maximum_fusion
  598.7 64.1 %while.11 = (s32[]{:T(128)}, bf16[12,1088,128]{2,1,0:T(8,128)(2,1)S(1)}, bf16[12,1088,128]{2,1,0:T(8,128)(2,1)}, bf16[12,1088,128]{2,1,0:T(8,128)(2,1)}, bf16[12...) while((s32[]{:T(128)}, bf16[12,1088,128]{2,1,0:T(8,128)(2,1)S(1)}, ...), condition=%wide.region_12.13_spmd.clone, body=%wide.region_9.12_spmd.clone.sunk | while | flops 615687232 | bytes 15631321 | solution.py:93
  668.4 4.6 all-to-all-start.2
  678.5 14.1 %all-to-all-done.2 = bf16[2,256,1536]{1,2,0:T(8,128)(2,1)} async-done(((bf16[2,256,1536]{1,2,0:T(8,128)(2,1)}), bf16[2,256,1536]{1,2,0:T(8,128)(2,1)}, u32[]{:S(2)}, u32[]{:S(2)}) %all-to-all-start.2) | async-done | bytes 1572896 | tf_op jit(solution)/shard_map/all_to_all | solution.py:134
  698.9 18.1 %all-to-all-done.3 = bf16[2,288,1536]{2,1,0:T(8,128)(2,1)S(1)} async-done(((bf16[2,288,1536]{2,1,0:T(8,128)(2,1)}), bf16[2,288,1536]{2,1,0:T(8,128)(2,1)S(1)}, u32[]{:S(2)}, u32[]{:S(2)}) %all-to-all-start.3) | async-done | bytes 1769504 | tf_op jit(solution)/shard_map/all_to_all | solution.py:135
  (153 shorter events, 152.5 us)
Async XLA Ops:
  7.2 202.8 %all-gather.7.cloned.1.call-start = ((), (), s32[]{:S(2)}) async-start(), calls=%async_computation.5 | async-start | bytes 30081024 | tf_op jit(solution)/shard_map/all_gather | solution.py:111
  65.9 289.6 %all-gather.11.cloned.1.call-start = ((), (), s32[]{:S(2)}) async-start(), calls=%async_computation.7 | async-start | bytes 30081024 | tf_op jit(solution)/shard_map/all_gather | solution.py:111
  117.2 2.3 copy-start.2
  118.6 1.6 copy-start.6
  118.7 283.9 %all-gather.5.cloned.1.call-start = ((), (), s32[]{:S(2)}) async-start(), calls=%async_computation.4 | async-start | bytes 4718592 | tf_op jit(solution)/shard_map/all_gather | solution.py:112
  120.9 2.6 copy-start
  123.5 329.9 %all-gather.9.cloned.1.call-start = ((), (), s32[]{:S(2)}) async-start(), calls=%async_computation.6 | async-start | bytes 5308416 | tf_op jit(solution)/shard_map/all_gather | solution.py:112
  124.5 6.0 copy-start.16
  496.5 3.9 copy-start.3
  496.5 3.9 copy-start.15
  500.4 1.6 copy-start.9
  500.4 1.6 copy-start.10
  542.2 5.8 copy-start.11
  542.2 5.8 copy-start.12
  542.2 5.8 copy-start.14
  548.1 4.2 copy-start.1
  548.1 4.2 copy-start.13
  552.3 2.0 copy-start.7
  552.3 2.0 copy-start.8
  594.6 4.1 copy-start.4
  662.8 1.7 copy-start.5
  668.4 24.2 %all-to-all-start.2 = ((bf16[2,256,1536]{1,2,0:T(8,128)(2,1)}), bf16[2,256,1536]{1,2,0:T(8,128)(2,1)}, u32[]{:S(2)}, u32[]{:S(2)}) async-start(bf16[2,256,1536]{1,2,0:T(8,128)(2,1)} %copy.49), calls=%async_computation.2 | async-start | bytes 3145728 | tf_op jit(solution)/shard_map/all_to_all | solution.py:134
  692.7 24.4 %all-to-all-start.3 = ((bf16[2,288,1536]{2,1,0:T(8,128)(2,1)}), bf16[2,288,1536]{2,1,0:T(8,128)(2,1)S(1)}, u32[]{:S(2)}, u32[]{:S(2)}) async-start(bf16[2,288,1536]{2,1,0:T(8,128)(2,1)} %all_to_all.61), calls=%async_computation.3 | async-start | bytes 3538944 | tf_op jit(solution)/shard_map/all_to_all | solution.py:135
Sparse Core Ops, SparseCore 0:
  66.0 143.9 all-gather.6
  212.1 143.3 all-gather.10
  357.7 44.9 all-gather.4
  404.0 49.3 all-gather.8
where the time goes:
time: 738 us; the launch traced here: 728 us
  waiting for transfers between devices  255 us (35%)
  local copies, waits for them, and re-layouts  183 us (25%)
  other arithmetic  96 us (13%)
  matrix products  89.9 us (12%)
  blocking collectives  80.5 us (11%)
  between operations  15.2 us (2%)
  starting transfers between devices  8.49 us (1%)
    all_gather x2, waiting for transfers between devices, on_device(): full_weight = lax.all_gather(relaid, 'rep', axis=0, tiled=True)  187 us
    all_to_all x2, blocking collectives, on_device(): lax.all_to_all(weights[stream], 'seq', split_axis=2, concat_axis=0, tiled...  80.5 us
    all_gather x2, local copies, waits for them, and re-layouts, on_device(): full_weight = lax.all_gather(relaid, 'rep', axis=0, tiled=True)  71.5 us
    dot_general x2, matrix products, on_device(): jnp.dot(all_rows, full_weight.reshape(D, 3 * col_count), preferred_elemen...  42.9 us
    all_gather x2, waiting for transfers between devices, on_device(): all_rows = lax.all_gather(modded, 'seq', axis=0, tiled=True)  35.3 us
    dot_general x12, matrix products, attend_head(): jnp.dot(softmax_out, value_head, preferred_element_type=jnp.float32)  24 us
    dot_general x12, matrix products, attend_head(): lax.dot_general(query_head, key_head, (((1,), (1,)), ((), ())), preferred...  22.9 us
    another operation x4, other arithmetic, rotate(): jnp.stack([first_part * cos_part - second_part * sin_part, first_part * s...  21 us
  transfers between devices with their start and end apart: 6, of which 6 were waited for; matrix products, arithmetic and copies ran while one was open for 18% of the time, Pallas kernels for 0%

commit v1 on v0

v1 whole, which is shorter than its diff:
```python
import functools

import jax
import jax.numpy as jnp
import numpy as np
from jax import lax
from jax.experimental import pallas as pl
from jax.experimental.pallas import tpu as pltpu
from jax.sharding import PartitionSpec as P

D = 3072
HEADS = 24
HD = 128
GRID = 24
TXT = 512
IMG = GRID * GRID
TOTAL = TXT + IMG
CHUNK = 32
KEYS = 9 * HD
ABSENT = -1e30
LOG2E = 1.4426950408889634


def head_groups(heads):
    if heads < 4:
        return [1] * heads
    return [heads - heads // 3, heads // 3]


def rope_image_tables():
    pair_count = HD // 2
    still_pairs = HD // 16
    row_pairs = (pair_count - still_pairs) // 2
    col_pairs = pair_count - still_pairs - row_pairs
    position = np.arange(IMG, dtype=np.int32)
    row_freq = np.float32(10000.0) ** (-np.arange(row_pairs, dtype=np.float32) / np.float32(row_pairs))
    col_freq = np.float32(10000.0) ** (-np.arange(col_pairs, dtype=np.float32) / np.float32(col_pairs))
    angles = np.concatenate(
        [
            np.zeros((IMG, still_pairs), np.float32),
            (position // GRID).astype(np.float32)[:, None] * row_freq[None, :].astype(np.float32),
            (position % GRID).astype(np.float32)[:, None] * col_freq[None, :].astype(np.float32),
        ],
        axis=1,
    ).astype(np.float64)
    cosine = np.repeat(np.cos(angles), 2, axis=1).astype(np.float32)
    sine = np.stack([-np.sin(angles), np.sin(angles)], axis=-1).reshape(IMG, HD).astype(np.float32)
    return cosine, sine


def modulate_kernel(step_index, table, text, image, text_out, image_out):
    for stream, tokens, out in ((0, text, text_out), (1, image, image_out)):
        values = tokens[...].astype(jnp.float32)
        center = values - jnp.mean(values, axis=-1, keepdims=True)
        spread = jnp.mean(center * center, axis=-1, keepdims=True)
        normed = center * lax.rsqrt(spread + 1e-06)
        shift_row = table[0, stream, 0:1, :]
        scale_row = table[0, stream, 1:2, :]
        out[...] = (normed * (1.0 + scale_row) + shift_row).astype(jnp.bfloat16)


def layer_modulate(time_index, mod_table, text, image):
    steps = 4 if text.shape[0] % 64 == 0 and image.shape[0] % 64 == 0 else 1
    steps = 2 if steps == 1 and text.shape[0] % 32 == 0 and image.shape[0] % 32 == 0 else steps
    rows = lambda x: pl.BlockSpec((x.shape[0] // steps, D), lambda i, step_index: (i, 0))
    return pl.pallas_call(
        modulate_kernel,
        grid_spec=pltpu.PrefetchScalarGridSpec(
            num_scalar_prefetch=1,
            grid=(steps,),
            in_specs=[
                pl.BlockSpec((1, 2, 2, D), lambda i, step_index: (step_index[0], 0, 0, 0)),
                rows(text),
                rows(image),
            ],
            out_specs=[rows(text), rows(image)],
        ),
        out_shape=[jax.ShapeDtypeStruct(x.shape, jnp.bfloat16) for x in (text, image)],
        compiler_params=pltpu.CompilerParams(vmem_limit_bytes=32 * 1024 * 1024),
    )(time_index, mod_table, text, image)


def swap_pairs(values):
    even = lax.broadcasted_iota(jnp.int32, values.shape, 1) % 2 == 0
    return jnp.where(even, pltpu.roll(values, HD - 1, 1), pltpu.roll(values, 1, 1))


def cut_kernel(groups, count, pair, columns, w, *rest):
    outs, sem = rest[:-1], rest[-1]
    copies = []
    for g, (first, heads) in enumerate(groups):
        for t in range(count):
            for h in range(heads):
                begin = pl.multiple_of(columns[t] + (first + h) * HD, HD)
                for s in range(2):
                    for part in range(3):
                        place = ((h // pair * 2 + s) * pair + h % pair) * 3 + part
                        copies.append(
                            pltpu.make_async_copy(
                                w.at[s, part, :, pl.ds(begin, HD)],
                                outs[g * count + t].at[:, pl.ds(place * HD, HD)],
                                sem.at[len(copies)],
                            )
                        )
    for copy in copies:
        copy.start()
    for copy in copies:
        copy.wait()


def cut_pieces(weights, columns, groups, pair):
    count = columns.shape[0]
    rows = weights.shape[2]
    outs = pl.pallas_call(
        functools.partial(cut_kernel, groups, count, pair),
        in_specs=[
            pl.BlockSpec(memory_space=pltpu.SMEM),
            pl.BlockSpec(memory_space=pltpu.HBM),
        ],
        out_specs=[pl.BlockSpec(memory_space=pltpu.VMEM)] * (len(groups) * count),
        out_shape=[
            jax.ShapeDtypeStruct((rows, 6 * heads * HD), jnp.bfloat16)
            for _, heads in groups
            for _ in range(count)
        ],
        scratch_shapes=[
            pltpu.SemaphoreType.DMA((6 * count * sum(heads for _, heads in groups),))
        ],
        compiler_params=pltpu.CompilerParams(vmem_limit_bytes=32 * 1024 * 1024),
    )(columns, weights)
    return [outs[g * count : (g + 1) * count] for g in range(len(groups))]


def stack_kernel(places, *rest):
    for i, piece in enumerate(rest[:-1]):
        rest[-1][places[i]] = piece[...]


def stack_pieces(pieces, places):
    in_vmem = pl.BlockSpec(memory_space=pltpu.VMEM)
    return pl.pallas_call(
        stack_kernel,
        in_specs=[pl.BlockSpec(memory_space=pltpu.SMEM)] + [in_vmem] * len(pieces),
        out_specs=in_vmem,
        out_shape=jax.ShapeDtypeStruct((len(pieces),) + pieces[0].shape, jnp.bfloat16),
        compiler_params=pltpu.CompilerParams(vmem_limit_bytes=32 * 1024 * 1024),
    )(places, *pieces)


def place_kernel(count, columns, *rest):
    pieces, sem = rest[:count], rest[-1]
    text, image = rest[-3], rest[-2]
    copies = []
    for i, piece in enumerate(pieces):
        width = piece.shape[1]
        begin = pl.multiple_of(columns[i], HD)
        start = 0
        for out in (text, image):
            rows = out.shape[0]
            copies.append(
                pltpu.make_async_copy(
                    piece.at[pl.ds(start, rows)],
                    out.at[:, pl.ds(begin, width)],
                    sem.at[len(copies)],
                )
            )
            start += rows
    for copy in copies:
        copy.start()
    for copy in copies:
        copy.wait()


def place_pieces(pieces, columns, outs, text_rows, image_rows):
    count = len(pieces)
    anywhere = pl.BlockSpec(memory_space=pl.ANY)
    return pl.pallas_call(
        functools.partial(place_kernel, count),
        in_specs=[pl.BlockSpec(memory_space=pltpu.SMEM)]
        + [pl.BlockSpec(memory_space=pltpu.VMEM)] * count
        + [anywhere] * len(outs),
        out_specs=[anywhere] * 2,
        out_shape=[
            jax.ShapeDtypeStruct((text_rows, D), jnp.bfloat16),
            jax.ShapeDtypeStruct((image_rows, D), jnp.bfloat16),
        ],
        scratch_shapes=[pltpu.SemaphoreType.DMA((2 * count,))],
        input_output_aliases={1 + count + i: i for i in range(len(outs))},
    )(columns, *pieces, *outs)


def project_stream(x, w, begin, samples, pair, gain, tables, q, k, v, flat):
    rows = x.shape[0] // samples
    flat[...] = jnp.dot(x[...], w, preferred_element_type=jnp.float32)
    for i in range(samples):
        for start in range(0, rows, CHUNK):
            mine = pl.ds(i * rows + start, CHUNK)
            here = pl.ds(begin + start, CHUNK)
            for h in range(pair):
                item = i * pair + h
                for part, target in ((0, q), (1, k)):
                    column = (h * 3 + part) * HD
                    values = flat[mine, column : column + HD]
                    power = jnp.mean(values * values, axis=-1, keepdims=True)
                    if begin == 0:
                        turned = values * gain[part : part + 1, :]
                    else:
                        angle = pl.ds(start, CHUNK)
                        a, b = tables[2 * part], tables[2 * part + 1]
                        turned = values * a[angle, :] + swap_pairs(values) * b[angle, :]
                    turned = turned * lax.rsqrt(power + 1e-06)
                    target[item, here, :HD] = turned.astype(jnp.bfloat16)
                column = (h * 3 + 2) * HD
                v[item, here, :HD] = flat[mine, column : column + HD].astype(jnp.bfloat16)


def attend_block(q, k, v, start, rows, write, score, prob, top):
    score[pl.ds(0, rows), :] = lax.dot_general(
        q[pl.ds(start, rows), :],
        k[...],
        (((1,), (1,)), ((), ())),
        preferred_element_type=jnp.float32,
    )
    for r in range(0, rows, CHUNK):
        row_max = jnp.max(score[pl.ds(r, CHUNK), :], axis=-1, keepdims=True)
        top[pl.ds(r, CHUNK), :] = jnp.broadcast_to(row_max, (CHUNK, HD))
    for r in range(0, rows, CHUNK):
        row_max = top[pl.ds(r, CHUNK), :]
        for tile in range(0, KEYS, HD):
            value = score[pl.ds(r, CHUNK), tile : tile + HD] - row_max
            prob[pl.ds(r, CHUNK), tile : tile + HD] = jnp.exp2(
                value * (HD ** (-0.5) * LOG2E)
            ).astype(jnp.bfloat16)
    mixed = jnp.dot(prob[pl.ds(0, rows), :], v[...], preferred_element_type=jnp.float32)
    write(start, rows, (mixed[:, :HD] / mixed[:, HD:]).astype(jnp.bfloat16))


def group_kernel(
    first, heads, which, pair, apart, rows_from, xt_far, xi_far, w, w_own,
    gain, aq, bq, ak, bk, mask, *rest
):
    samples = len(which)
    steps = heads // pair
    items = samples * pair
    count = samples * 2 if apart else samples
    outs = rest[:count]
    xt, xi, buffers, q_s, k_s, v_s, flat_t, flat_i, scores, probs, tops, sems = rest[count:]
    tables = (aq, bq, ak, bk)
    slots = min(steps, 2)
    width = pair * 3 * HD

    def fetch(h, slot, stream):
        begin = pl.multiple_of((h * 2 + stream) * width, width)
        target = buffers.at[slot, stream]
        if rows_from is None:
            return [
                pltpu.make_async_copy(
                    w.at[:, pl.ds(begin, width)], target, sems.at[2 + slot * 2 + stream]
                )
            ]
        count = rows_from.shape[0]
        copies = []
        for n in range(count):
            if n == 0:
                begin_own = pl.multiple_of(
                    ((first // pair + h) * 2 + stream) * width, width
                )
                part = w_own.at[:, :, :, pl.ds(begin_own, width)]
            else:
                part = w.at[:, :, n - 1, :, pl.ds(begin, width)]
            copies.append(
                pltpu.make_async_copy(
                    part,
                    target.at[:, rows_from[n, 0], :, rows_from[n, 1], :, :],
                    sems.at[2 + (slot * 2 + stream) * count + n],
                )
            )
        return copies

    def start(copies):
        for copy in copies:
            copy.start()

    def wait(copies):
        for copy in copies:
            copy.wait()

    tokens = [
        pltpu.make_async_copy(far.at[pl.ds(which[0] * rows, samples * rows)], near, sems.at[n])
        for n, (far, near, rows) in enumerate(((xt_far, xt, TXT), (xi_far, xi, IMG)))
    ]
    for stream in range(2):
        start(fetch(0, 0, stream))
        tokens[stream].start()
    lead = lax.broadcasted_iota(jnp.int32, (KEYS, HD), 1) == 0
    for slot in range(slots):
        for i in range(items):
            q_s[slot, i, :, HD:] = jnp.where(lead, 1.0, 0.0).astype(jnp.bfloat16)
            k_s[slot, i, :, HD:] = mask[which[i // pair]]
            k_s[slot, i, TOTAL:, :HD] = jnp.zeros((KEYS - TOTAL, HD), jnp.bfloat16)
            v_s[slot, i, :, HD:] = jnp.ones((KEYS, HD), jnp.bfloat16)
            v_s[slot, i, TOTAL:, :HD] = jnp.zeros((KEYS - TOTAL, HD), jnp.bfloat16)

    def project(h, stream):
        slot = h % 2
        project_stream(
            (xt, xi)[stream],
            buffers[slot, stream].reshape(D, width),
            0 if stream == 0 else TXT,
            samples,
            pair,
            gain,
            tables,
            q_s.at[slot],
            k_s.at[slot],
            v_s.at[slot],
            (flat_t, flat_i)[stream],
        )

    def attend(h, i):
        slot = h % 2

        def write(start, rows, block):
            column = (h * pair + i % pair) * HD
            column = column if isinstance(h, int) else pl.multiple_of(column, HD)
            if apart:
                begin = 0 if start < TXT else TXT // 2
                for k in range(2):
                    half = block[k * rows // 2 : (k + 1) * rows // 2]
                    outs[2 * (i // pair) + k][pl.ds(begin, rows // 2), pl.ds(column, HD)] = half
            else:
                outs[i // pair][pl.ds(start, rows), pl.ds(column, HD)] = block

        for n, (start, rows) in enumerate(((0, TXT), (TXT, IMG))):
            attend_block(
                q_s.at[slot, i],
                k_s.at[slot, i],
                v_s.at[slot, i],
                start,
                rows,
                write,
                scores.at[n],
                probs.at[n],
                tops.at[n],
            )

    for stream in range(2):
        wait(fetch(0, 0, stream))
        tokens[stream].wait()
        if steps > 1:
            start(fetch(1, 1, stream))
        project(0, stream)

    def step(h, carry):
        for stream in range(2):
            wait(fetch(h, h % 2, stream))

        @pl.when(h + 1 < steps)
        def _():
            for stream in range(2):
                start(fetch(h + 1, (h + 1) % 2, stream))

        half = max(items // 2, 1)
        project(h, 0)
        for i in range(half):
            attend(h - 1, i)
        project(h, 1)
        for i in range(half, items):
            attend(h - 1, i)
        return carry

    if steps > 1:
        lax.fori_loop(1, steps, step, 0)
    for i in range(items):
        attend(steps - 1, i)


def attend_group(xt, xi, gathered, own, rows_from, tables, mask, first, heads, which, pair, apart):
    samples = len(which)
    count = samples * 2 if apart else samples
    rows = TOTAL // 2 if apart else TOTAL
    slots = min(heads // pair, 2)
    in_vmem = pl.BlockSpec(memory_space=pltpu.VMEM)
    in_hbm = pl.BlockSpec(memory_space=pltpu.HBM)
    kernel = functools.partial(group_kernel, first, heads, which, pair, apart)
    if own is None:
        weight_args, weight_specs, buffer, quarters = [gathered], [in_hbm], (D,), 1
        body = lambda xt, xi, w, *rest: kernel(None, xt, xi, w, None, *rest)
    else:
        outers, cores, _, weight_rows, _ = gathered.shape
        quarters = rows_from.shape[0]
        ranks = quarters // 2
        weight_args = [gathered, own, rows_from]
        weight_specs = [in_hbm, in_hbm, pl.BlockSpec(memory_space=pltpu.SMEM)]
        buffer = (outers, 2, cores, ranks, weight_rows)
        body = lambda xt, xi, w, w_own, places, *rest: kernel(places, xt, xi, w, w_own, *rest)
    return pl.pallas_call(
        body,
        in_specs=[in_hbm] * 2 + weight_specs + [in_vmem] * (len(tables) + 1),
        out_specs=[in_vmem] * count,
        out_shape=[jax.ShapeDtypeStruct((rows, heads * HD), jnp.bfloat16)] * count,
        scratch_shapes=[
            pltpu.VMEM((samples * TXT, D), jnp.bfloat16),
            pltpu.VMEM((samples * IMG, D), jnp.bfloat16),
            pltpu.VMEM((slots, 2) + buffer + (pair * 3 * HD,), jnp.bfloat16),
        ]
        + [pltpu.VMEM((slots, samples * pair, KEYS, 2 * HD), jnp.bfloat16)] * 3
        + [
            pltpu.VMEM((samples * TXT, pair * 3 * HD), jnp.float32),
            pltpu.VMEM((samples * IMG, pair * 3 * HD), jnp.float32),
            pltpu.VMEM((2, IMG, KEYS), jnp.float32),
            pltpu.VMEM((2, IMG, KEYS), jnp.bfloat16),
            pltpu.VMEM((2, IMG, HD), jnp.float32),
            pltpu.SemaphoreType.DMA((2 + 2 * slots * quarters,)),
        ],
        compiler_params=pltpu.CompilerParams(vmem_limit_bytes=56 * 1024 * 1024),
        cost_estimate=pl.CostEstimate(
            flops=samples * heads * (2 * TOTAL * D * 3 * HD + 8 * TOTAL * TOTAL * HD),
            bytes_accessed=heads * D * 6 * HD * 2 + 2 * samples * TOTAL * D,
            transcendentals=samples * heads * TOTAL * TOTAL,
        ),
    )(xt, xi, *weight_args, *tables, mask)


def on_device(text_tokens, image_tokens, weights, qk_gain, mod_table, text_lengths, time_index):
    ranks = lax.axis_size("seq")
    reps = lax.axis_size("rep")
    split = 2 if (HEADS // ranks) % 2 == 0 and reps % 4 == 0 else 1
    cores = 2
    outers = reps // (split * cores)
    rank = lax.axis_index("seq")
    rep = lax.axis_index("rep")
    core = lax.rem(rep, cores)
    f_here = lax.rem(rep // cores, split)
    heads_here = HEADS // (split * ranks)
    cols = heads_here * HD
    weight_rows = weights.shape[1]
    text_rows = text_tokens.shape[1]
    image_rows = image_tokens.shape[1]
    weights = weights.transpose(0, 2, 1, 3)

    def permute(value, target):
        pairs = []
        for o in range(outers):
            for f in range(split):
                for c in range(cores):
                    for r in range(ranks):
                        tf, tc, tr = target(f, c, r)
                        pairs.append(
                            (
                                ((o * split + f) * cores + c) * ranks + r,
                                ((o * split + tf) * cores + tc) * ranks + tr % ranks,
                            )
                        )
        return lax.ppermute(value, ("rep", "seq"), pairs)

    def shift(value, flip, k):
        if flip == 0 and k % ranks == 0:
            return value
        return permute(value, lambda f, c, r: (f ^ flip, c, r + k))

    def source(k):
        return lax.rem(rank - k + ranks, ranks)

    def head_owner(flip, k):
        f = f_here ^ flip if split > 1 else 0
        return f * ranks + lax.rem(rank + k, ranks)

    groups = []
    first = 0
    for heads in head_groups(heads_here):
        groups.append((first, heads))
        first += heads
    pair = 2 if all(first % 2 == 0 and heads % 2 == 0 for first, heads in groups) else 1
    hops = [(a, k) for a in range(split) for k in range(ranks)]
    targets = jnp.stack([head_owner(a, k) * cols for a, k in hops]).astype(jnp.int32)
    places = jnp.stack([source(k) for _, k in hops]).astype(jnp.int32)
    rows_from = None
    if split > 1:
        rows_from = jnp.stack(
            [jnp.stack([f_here ^ a, source(k)]) for a, k in hops]
        ).astype(jnp.int32)
        own_columns = cut_pieces(weights, targets[:1], [(0, heads_here)], pair)[0][0]
        targets, own_columns = lax.optimization_barrier((targets[1:], own_columns))
        hops = hops[1:]
        places = jnp.arange(len(hops), dtype=jnp.int32)
    blocks = []
    for pieces in cut_pieces(weights, targets, groups, pair):
        pieces = [shift(piece, a, k) for piece, (a, k) in zip(pieces, hops)]
        block = stack_pieces(pieces, places)
        blocks.append(block.reshape(len(hops) * weight_rows, block.shape[-1]))

    gather_groups = [
        [(o * split + f) * cores + c for o in range(outers) for c in range(cores)]
        for f in range(split)
    ]

    def gather(block):
        return lax.all_gather(
            block,
            "rep",
            axis=0,
            tiled=True,
            axis_index_groups=gather_groups if split > 1 else None,
        )

    own_weight = gather(own_columns) if split > 1 else None
    modded = layer_modulate(time_index, mod_table, text_tokens[0], image_tokens[0])
    modded, blocks = lax.optimization_barrier((modded, blocks))
    own = [[shift(m, 0, k) for k in range(ranks)] for m in modded]
    other_image = shift(modded[1], 1, 0) if split > 1 else modded[1]
    texts, images = own
    if split > 1:
        texts = texts + [shift(piece, 1, 0) for piece in own[0]]
        images = images + [shift(other_image, 0, k) for k in range(ranks)]
    texts, images = [jnp.concatenate(pieces, axis=0) for pieces in (texts, images)]

    apart = ranks == 2
    order = [source(k) for k in range(ranks)]
    cosine_np, sine_np = rope_image_tables()

    def reorder(table):
        table = jnp.asarray(table)
        return jnp.concatenate(
            [lax.dynamic_slice_in_dim(table, r * image_rows, image_rows, 0) for r in order], axis=0
        )

    cosine, sine = reorder(cosine_np), reorder(sine_np)
    swapped = qk_gain.reshape(2, 2, HD // 2, 2)[..., ::-1].reshape(2, 2, HD)
    tables = [qk_gain[0]]
    for part in range(2):
        tables += [cosine * qk_gain[1, part], sine * swapped[1, part]]
    within = jnp.arange(text_rows, dtype=jnp.int32)
    masks = []
    for flip in range(split):
        live = shift(text_lengths, flip, 0)[0]
        column = [
            jnp.where(r * text_rows + within < live, 0.0, ABSENT).astype(jnp.float32)
            for r in order
        ]
        column.append(jnp.zeros((IMG,), jnp.float32))
        column.append(jnp.full((KEYS - TOTAL,), ABSENT, jnp.float32))
        masks.append(jnp.concatenate(column))
    mask = jnp.where(jnp.arange(HD) == 0, jnp.stack(masks)[:, :, None], 0.0).astype(jnp.bfloat16)

    blocks[-1], texts, images, tables, mask = lax.optimization_barrier(
        (blocks[-1], texts, images, tables, mask)
    )

    def attend(weight, first, heads):
        if split > 1:
            weight = weight.reshape(outers, cores, len(hops), weight_rows, weight.shape[-1])
        received, columns = [], []
        for flip in reversed(range(split)):
            parts = attend_group(
                texts, images, weight, own_quarter, rows_from, tables, mask,
                first, heads, (flip,), pair, apart,
            )
            weight, parts = lax.optimization_barrier((weight, parts))
            if not apart:
                whole = parts[0]
                parts = []
                for k in range(ranks):
                    text = whole[k * text_rows : (k + 1) * text_rows]
                    image = whole[TXT + k * image_rows : TXT + (k + 1) * image_rows]
                    parts.append(jnp.concatenate([text, image], axis=0))
            for k in range(ranks):
                received.append(shift(parts[k], flip, ranks - k))
                columns.append(head_owner(flip, k) * cols + first * HD)
        return received, columns

    def place(received, columns, outs):
        columns = jnp.stack(columns).astype(jnp.int32)
        return place_pieces(received, columns, outs, text_rows, image_rows)

    outs = []
    if split > 1:
        blocks[0], own_weight = lax.optimization_barrier((blocks[0], own_weight))
    weight = gather(blocks[0])
    own_quarter = None
    if split > 1:
        own_quarter = own_weight.reshape(outers, cores, weight_rows, own_weight.shape[-1])
    for g, (first, heads) in enumerate(groups):
        if g + 1 < len(groups):
            block, weight = lax.optimization_barrier((blocks[g + 1], weight))
            following = gather(block)
        outs = place(*attend(weight, first, heads), outs)
        weight = following
    return (outs[0][None], outs[1][None])


def solution(mesh):
    placed = (
        P("rep", "seq", None),
        P("rep", "seq", None),
        P(None, ("rep", "seq"), None, None),
        P(),
        P(),
        P("rep"),
        P("rep"),
    )
    return jax.shard_map(
        on_device,
        mesh=mesh,
        in_specs=placed,
        out_specs=(P("rep", "seq", None), P("rep", "seq", None)),
        check_vma=False,
    )
```

time: 738 us -> 354 us (0.48)
  local copies, waits for them, and re-layouts: 183 us -> 14.9 us
  Pallas kernels: 0 us -> 108 us
  waiting for transfers between devices: 255 us -> 164 us
  matrix products: 89.9 us -> 0 us
  blocking collectives: 80.5 us -> 0 us
  other arithmetic: 96 us -> 19.4 us
  starting transfers between devices: 8.49 us -> 26.8 us
    all_gather x4 -> x3, waiting for transfers between devices: 223 us -> 36.8 us  [gather(): lax.all_gather(block, 'rep', axis=0, tiled=True, axis_index_groups=gather...]
    ppermute x0 -> x19, waiting for transfers between devices: none -> 127 us  [permute(): return lax.ppermute(value, ('rep', 'seq'), pairs)]
    pallas_call x0 -> x11, Pallas kernels: none -> 108 us  [the longest x4 93.7 us: attend_group(): pl.pallas_call(body, in_specs=[in_hbm] * 2 + weight_specs + [in_vmem] * (...]
    dot_general x26 -> x0, matrix products: 89.9 us -> none  [the longest x2 42.9 us: on_device(): jnp.dot(all_rows, full_weight.reshape(D, 3 * col_count), preferred_elemen...]
    all_to_all x2 -> x0, blocking collectives: 80.5 us -> none  [on_device(): lax.all_to_all(weights[stream], 'seq', split_axis=2, concat_axis=0, tiled...]
    all_gather x2 -> x0, local copies, waits for them, and re-layouts: 71.5 us -> none  [on_device(): full_weight = lax.all_gather(relaid, 'rep', axis=0, tiled=True)]
    another operation x6 -> x7, other arithmetic: 41.3 us -> 2.05 us  [the longest x2 1.2 us: place(): columns = jnp.stack(columns).astype(jnp.int32)]
    all_to_all x2 -> x0, waiting for transfers between devices: 32.3 us -> none  [the longest x1 18.1 us: on_device(): lax.all_to_all(joined[TXT:], 'seq', split_axis=0, concat_axis=1, tiled=True)]
  transfers between devices with their start and end apart: 6 -> 22, of which waited for: 6 -> 11; matrix products, arithmetic and copies ran while one was open for 18% -> 7% of each run, Pallas kernels for 0% -> 30%
where the time goes in v1:
time: 354 us; the launch traced here: 348 us
  waiting for transfers between devices  164 us (46%)
  Pallas kernels  108 us (31%)
  starting transfers between devices  26.8 us (8%)
  other arithmetic  19.4 us (5%)
  between operations  15.8 us (4%)
  local copies, waits for them, and re-layouts  14.9 us (4%)
    ppermute x19, waiting for transfers between devices, permute(): return lax.ppermute(value, ('rep', 'seq'), pairs)  127 us
    pallas_call x4, Pallas kernels, attend_group(): pl.pallas_call(body, in_specs=[in_hbm] * 2 + weight_specs + [in_vmem] * (...  93.7 us
    all_gather x3, waiting for transfers between devices, gather(): lax.all_gather(block, 'rep', axis=0, tiled=True, axis_index_groups=gather...  36.8 us
    ppermute x19, starting transfers between devices, permute(): return lax.ppermute(value, ('rep', 'seq'), pairs)  26.7 us
    concatenate x2, other arithmetic, on_device(): jnp.concatenate(pieces, axis=0)  11.8 us
    unnamed x30, local copies, waits for them, and re-layouts  10.3 us
  transfers between devices with their start and end apart: 22, of which 11 were waited for; matrix products, arithmetic and copies ran while one was open for 7% of the time, Pallas kernels for 30%

profile of v1, /device:TPU:0, one launch (start us, length us, event | category | flops | bytes accessed | tf_op | source)
XLA Modules:
  0.0 348.4 jit_solution(555748843541267637)
XLA Ops:
  7.3 2.0 copy-done
  11.6 2.5 shard_map.106
  14.0 3.0 collective-permute-start.3
  17.1 2.0 collective-permute-start.1
  20.5 1.5 collective-permute-start.4
  22.1 2.8 collective-permute-done.3.rest_0_
  24.9 3.0 collective-permute-start.5
  32.8 2.5 shard_map.104
  35.3 21.9 %collective-permute-done.4.rest_1_ = bf16[96,1536]{1,0:T(8,128)(2,1)S(1)} collective-permute-done((bf16[96,1536]{1,0:T(8,128)(2,1)S(1)}, bf16[96,1536]{1,0:T(8,128)(2,1)S(1)}, u32[]{:S(2)}, u32[]{:S(2)}) %collective-permute-start.4) | collective-permute-done | bytes 294944 | tf_op jit(solution)/shard_map/ppermute | solution.py:455
  58.7 1.9 shard_map.107
  60.6 24.5 %all-gather.4.cloned.1.call-done = bf16[768,4608]{1,0:T(8,128)(2,1)} async-done(((bf16[96,4608]{1,0:T(8,128)(2,1)}), bf16[768,4608]{1,0:T(8,128)(2,1)}) %all-gather.4.cloned.1.call-update) | async-done | bytes 7077904 | tf_op jit(solution)/shard_map/all_gather | solution.py:499
  85.1 1.5 collective-permute-start.6
  92.7 29.1 %collective-permute-done.6 = bf16[256,3072]{1,0:T(8,128)(2,1)} collective-permute-done((bf16[256,3072]{1,0:T(8,128)(2,1)S(1)}, bf16[256,3072]{1,0:T(8,128)(2,1)}, u32[]{:S(2)}, u32[]{:S(2)}) %collective-permute-start.6) | collective-permute-done | bytes 1572896 | tf_op jit(solution)/shard_map/ppermute | solution.py:455
  123.3 1.9 constant_dynamic-slice_fusion.1
  125.9 1.8 fusion
  129.9 1.8 fusion.2
  133.7 28.3 %collective-permute-done.7 = bf16[256,3072]{1,0:T(8,128)(2,1)} collective-permute-done((bf16[256,3072]{1,0:T(8,128)(2,1)S(1)}, bf16[256,3072]{1,0:T(8,128)(2,1)}, u32[]{:S(2)}, u32[]{:S(2)}) %collective-permute-start.7) | collective-permute-done | bytes 1572896 | tf_op jit(solution)/shard_map/ppermute | solution.py:455
  162.0 32.7 %collective-permute-done.8 = bf16[256,3072]{1,0:T(8,128)(2,1)} collective-permute-done((bf16[256,3072]{1,0:T(8,128)(2,1)}, bf16[256,3072]{1,0:T(8,128)(2,1)}, u32[]{:S(2)}, u32[]{:S(2)}) %collective-permute-start.8) | collective-permute-done | bytes 1572896 | tf_op jit(solution)/shard_map/ppermute | solution.py:455
  194.7 5.7 %pad_maximum_fusion.1.xt = bf16[1024,3072]{1,0:T(8,128)(2,1)} fusion(bf16[256,3072]{1,0:T(8,128)(2,1)} %collective-permute-done.8, bf16[256,3072]{1,0:T(8,128)(2,1)} %collective-permute-done.7, bf16[256,3072]{1,0:T(8,128)(2,1)} %collective-permute-done.6, bf16[256,3072]{1,0:T(8,128)(2,1)S(1)} %get-tuple-element.61), kind=kLoop, calls=%fused_computation.1 | loop fusion | flops 25165824 | bytes 12582912 | tf_op jit(solution)/shard_map/concatenate | solution.py:516
  200.4 5.0 %collective-permute-done.11 = bf16[288,3072]{1,0:T(8,128)(2,1)} collective-permute-done((bf16[288,3072]{1,0:T(8,128)(2,1)}, bf16[288,3072]{1,0:T(8,128)(2,1)}, u32[]{:S(2)}, u32[]{:S(2)}) %collective-permute-start.11) | collective-permute-done | bytes 1769504 | tf_op jit(solution)/shard_map/ppermute | solution.py:455
  205.4 6.1 %pad_maximum_fusion.xi = bf16[1152,3072]{1,0:T(8,128)(2,1)} fusion(bf16[288,3072]{1,0:T(8,128)(2,1)} %collective-permute-done.11, bf16[288,3072]{1,0:T(8,128)(2,1)} %collective-permute-done.10, bf16[288,3072]{1,0:T(8,128)(2,1)} %collective-permute-done.9, bf16[288,3072]{1,0:T(8,128)(2,1)S(1)} %get-tuple-element.62), kind=kLoop, calls=%fused_computation | loop fusion | flops 28311552 | bytes 14155776 | tf_op jit(solution)/shard_map/concatenate | solution.py:516
  211.5 4.0 %all-gather.6.cloned.1.call-done = bf16[2304,3072]{1,0:T(8,128)(2,1)} async-done(((bf16[288,3072]{1,0:T(8,128)(2,1)}), bf16[2304,3072]{1,0:T(8,128)(2,1)}) %all-gather.6.cloned.1.call-update) | async-done | bytes 14155792 | tf_op jit(solution)/shard_map/all_gather | solution.py:499
  216.3 29.4 %shard_map.111 = (bf16[544,512]{1,0:T(8,128)(2,1)}, bf16[544,512]{1,0:T(8,128)(2,1)}) custom-call(bf16[1024,3072]{1,0:T(8,128)(2,1)} %pad_maximum_fusion.1.xt, bf16[1152,3072]{1,0:T(8,128)(2,1)} %pad_maximum_fusion.xi, bf16[4,2,3,96,3072]{4,3,2,1,0:T(8,128)(2,1)} %bitcast.57, bf16[4,2,96,4608]{3,2,1,0:T(8,128)(2,1)} %bitcast.49, s32[4,2]{1,0:T(4,128)} %pad_add_fusion.places, ...), custom_call_target="tpu_custom_call" | custom-call | flops 15116271616 | bytes 25559040 | tf_op jit(solution)/shard_map/pallas_call | solution.py:397
  245.7 29.6 %shard_map.112 = (bf16[544,512]{1,0:T(8,128)(2,1)}, bf16[544,512]{1,0:T(8,128)(2,1)}) custom-call(bf16[1024,3072]{1,0:T(8,128)(2,1)} %pad_maximum_fusion.1.xt, bf16[1152,3072]{1,0:T(8,128)(2,1)} %pad_maximum_fusion.xi, bf16[4,2,3,96,3072]{4,3,2,1,0:T(8,128)(2,1)} %bitcast.58, bf16[4,2,96,4608]{3,2,1,0:T(8,128)(2,1)} %bitcast.50, s32[4,2]{1,0:T(4,128)} %pad_add_fusion.places, ...), custom_call_target="tpu_custom_call" | custom-call | flops 15116271616 | bytes 25559040 | tf_op jit(solution)/shard_map/pallas_call | solution.py:397
  275.3 1.5 collective-permute-start.18
  278.9 8.4 %all-gather.8.cloned.1.call-done = bf16[2304,1536]{1,0:T(8,128)(2,1)} async-done(((bf16[288,1536]{1,0:T(8,128)(2,1)}), bf16[2304,1536]{1,0:T(8,128)(2,1)}) %all-gather.8.cloned.1.call-update) | async-done | bytes 7077904 | tf_op jit(solution)/shard_map/all_gather | solution.py:499
  287.3 17.5 %shard_map.109 = (bf16[544,256]{1,0:T(8,128)(2,1)}, bf16[544,256]{1,0:T(8,128)(2,1)}) custom-call(bf16[1024,3072]{1,0:T(8,128)(2,1)} %pad_maximum_fusion.1.xt, bf16[1152,3072]{1,0:T(8,128)(2,1)} %pad_maximum_fusion.xi, bf16[4,2,3,96,1536]{4,3,2,1,0:T(8,128)(2,1)} %bitcast.53, bf16[4,2,96,4608]{3,2,1,0:T(8,128)(2,1)} %bitcast.51, s32[4,2]{1,0:T(4,128)} %pad_add_fusion.places, ...), custom_call_target="tpu_custom_call" | custom-call | flops 7558135808 | bytes 16121856 | tf_op jit(solution)/shard_map/pallas_call | solution.py:397
  304.7 17.3 %shard_map.110 = (bf16[544,256]{1,0:T(8,128)(2,1)}, bf16[544,256]{1,0:T(8,128)(2,1)}) custom-call(bf16[1024,3072]{1,0:T(8,128)(2,1)} %pad_maximum_fusion.1.xt, bf16[1152,3072]{1,0:T(8,128)(2,1)} %pad_maximum_fusion.xi, bf16[4,2,3,96,1536]{4,3,2,1,0:T(8,128)(2,1)} %bitcast.54, bf16[4,2,96,4608]{3,2,1,0:T(8,128)(2,1)} %bitcast.52, s32[4,2]{1,0:T(4,128)} %pad_add_fusion.places, ...), custom_call_target="tpu_custom_call" | custom-call | flops 7558135808 | bytes 16121856 | tf_op jit(solution)/shard_map/pallas_call | solution.py:397
  322.0 1.5 collective-permute-start.15
  328.5 3.0 shard_map.113
  331.8 6.5 %collective-permute-done.13.rest_0_ = bf16[544,256]{1,0:T(8,128)(2,1)S(1)} collective-permute-done((bf16[544,256]{1,0:T(8,128)(2,1)}, bf16[544,256]{1,0:T(8,128)(2,1)S(1)}, u32[]{:S(2)}, u32[]{:S(2)}) %collective-permute-start.13) | collective-permute-done | bytes 278560 | tf_op jit(solution)/shard_map/ppermute | solution.py:455
  339.1 2.3 shard_map.114
  (86 shorter events, 30.2 us)
Async XLA Ops:
  7.2 77.9 %all-gather.4.cloned.1.call-start = ((), (), s32[]{:S(2)}) async-start(), calls=%async_computation | async-start | bytes 7962624 | tf_op jit(solution)/shard_map/all_gather | solution.py:499
  7.2 2.0 copy-start
  9.2 2.3 copy-start.1
  10.9 204.6 %all-gather.6.cloned.1.call-start = ((), (), s32[]{:S(2)}) async-start(), calls=%async_computation.1 | async-start | bytes 15925248 | tf_op jit(solution)/shard_map/all_gather | solution.py:499
  14.0 74.7 %copy-start.12 = (f32[2,2,128]{2,1,0:T(2,128)S(1)}, f32[2,2,128]{2,1,0:T(2,128)}, u32[]{:S(2)}) copy-start(f32[2,2,128]{2,1,0:T(2,128)} %param.12) | copy-start | bytes 6148
  14.0 10.8 %collective-permute-start.3 = (bf16[96,1536]{1,0:T(8,128)(2,1)S(1)}, bf16[96,1536]{1,0:T(8,128)(2,1)S(1)}, u32[]{:S(2)}, u32[]{:S(2)}) collective-permute-start(bf16[96,1536]{1,0:T(8,128)(2,1)S(1)} %get-tuple-element.57), channel_id=1, source_target_pairs={{0,1},{1,0},{2,3},{3,2},{4,5},{5,4},{6,7},{7,6},{8,9},{9,8},{10,11... | collective-permute-start | bytes 884744 | tf_op jit(solution)/shard_map/ppermute | solution.py:455
  17.0 41.7 %collective-permute-start = (bf16[96,3072]{1,0:T(8,128)(2,1)S(1)}, bf16[96,3072]{1,0:T(8,128)(2,1)S(1)}, u32[]{:S(2)}, u32[]{:S(2)}) collective-permute-start(bf16[96,3072]{1,0:T(8,128)(2,1)S(1)} %get-tuple-element.54), channel_id=1, source_target_pairs={{0,1},{1,0},{2,3},{3,2},{4,5},{5,4},{6,7},{7,6},{8,9},{9,8},{10,11... | collective-permute-start | bytes 1769480 | tf_op jit(solution)/shard_map/ppermute | solution.py:455
  17.1 41.6 %collective-permute-start.1 = (bf16[96,3072]{1,0:T(8,128)(2,1)S(1)}, bf16[96,3072]{1,0:T(8,128)(2,1)S(1)}, u32[]{:S(2)}, u32[]{:S(2)}) collective-permute-start(bf16[96,3072]{1,0:T(8,128)(2,1)S(1)} %get-tuple-element.55), channel_id=1, source_target_pairs={{0,4},{1,5},{2,6},{3,7},{4,0},{5,1},{6,2},{7,3},{8,12},{9,13},{10,... | collective-permute-start | bytes 1769480 | tf_op jit(solution)/shard_map/ppermute | solution.py:455
  19.1 39.6 %collective-permute-start.2 = (bf16[96,3072]{1,0:T(8,128)(2,1)S(1)}, bf16[96,3072]{1,0:T(8,128)(2,1)S(1)}, u32[]{:S(2)}, u32[]{:S(2)}) collective-permute-start(bf16[96,3072]{1,0:T(8,128)(2,1)S(1)} %get-tuple-element.56), channel_id=1, source_target_pairs={{0,5},{1,4},{2,7},{3,6},{4,1},{5,0},{6,3},{7,2},{8,13},{9,12},{10,... | collective-permute-start | bytes 1769480 | tf_op jit(solution)/shard_map/ppermute | solution.py:455
  20.5 36.7 %collective-permute-start.4 = (bf16[96,1536]{1,0:T(8,128)(2,1)S(1)}, bf16[96,1536]{1,0:T(8,128)(2,1)S(1)}, u32[]{:S(2)}, u32[]{:S(2)}) collective-permute-start(bf16[96,1536]{1,0:T(8,128)(2,1)S(1)} %get-tuple-element.58), channel_id=1, source_target_pairs={{0,4},{1,5},{2,6},{3,7},{4,0},{5,1},{6,2},{7,3},{8,12},{9,13},{10,... | collective-permute-start | bytes 884744 | tf_op jit(solution)/shard_map/ppermute | solution.py:455
  24.9 32.3 %collective-permute-start.5 = (bf16[96,1536]{1,0:T(8,128)(2,1)S(1)}, bf16[96,1536]{1,0:T(8,128)(2,1)S(1)}, u32[]{:S(2)}, u32[]{:S(2)}) collective-permute-start(bf16[96,1536]{1,0:T(8,128)(2,1)S(1)} %get-tuple-element.59), channel_id=1, source_target_pairs={{0,5},{1,4},{2,7},{3,6},{4,1},{5,0},{6,3},{7,2},{8,13},{9,12},{10,... | collective-permute-start | bytes 884744 | tf_op jit(solution)/shard_map/ppermute | solution.py:455
  28.5 1.5 copy-start.3
  30.0 1.4 copy-start.4
  31.5 1.4 copy-start.5
  85.1 202.2 %all-gather.8.cloned.1.call-start = ((), (), s32[]{:S(2)}) async-start(), calls=%async_computation.2 | async-start | bytes 7962624 | tf_op jit(solution)/shard_map/all_gather | solution.py:499
  85.1 36.7 %collective-permute-start.6 = (bf16[256,3072]{1,0:T(8,128)(2,1)S(1)}, bf16[256,3072]{1,0:T(8,128)(2,1)}, u32[]{:S(2)}, u32[]{:S(2)}) collective-permute-start(bf16[256,3072]{1,0:T(8,128)(2,1)S(1)} %get-tuple-element.61), channel_id=1, source_target_pairs={{0,1},{1,0},{2,3},{3,2},{4,5},{5,4},{6,7},{7,6},{8,9},{9,8},{10,11... | collective-permute-start | bytes 4718600 | tf_op jit(solution)/shard_map/ppermute | solution.py:455
  86.7 42.5 %collective-permute-start.10 = (bf16[288,3072]{1,0:T(8,128)(2,1)S(1)}, bf16[288,3072]{1,0:T(8,128)(2,1)}, u32[]{:S(2)}, u32[]{:S(2)}) collective-permute-start(bf16[288,3072]{1,0:T(8,128)(2,1)S(1)} %get-tuple-element.62), channel_id=1, source_target_pairs={{0,4},{1,5},{2,6},{3,7},{4,0},{5,1},{6,2},{7,3},{8,12},{9,13},{10,... | collective-permute-start | bytes 5308424 | tf_op jit(solution)/shard_map/ppermute | solution.py:455
  88.1 43.5 %collective-permute-start.12 = (s32[1]{0:T(128)}, s32[1]{0:T(128)}, u32[]{:S(2)}, u32[]{:S(2)}) collective-permute-start(s32[1]{0:T(128)} %param.14), channel_id=1, source_target_pairs={{0,4},{1,5},{2,6},{3,7},{4,0},{5,1},{6,2},{7,3},{8,12},{9,13},{10,... | collective-permute-start | bytes 20 | tf_op jit(solution)/shard_map/ppermute | solution.py:455
  91.2 70.7 %collective-permute-start.7 = (bf16[256,3072]{1,0:T(8,128)(2,1)S(1)}, bf16[256,3072]{1,0:T(8,128)(2,1)}, u32[]{:S(2)}, u32[]{:S(2)}) collective-permute-start(bf16[256,3072]{1,0:T(8,128)(2,1)S(1)} %get-tuple-element.61), channel_id=1, source_target_pairs={{0,4},{1,5},{2,6},{3,7},{4,0},{5,1},{6,2},{7,3},{8,12},{9,13},{10,... | collective-permute-start | bytes 4718600 | tf_op jit(solution)/shard_map/ppermute | solution.py:455
  121.8 72.8 %collective-permute-start.8 = (bf16[256,3072]{1,0:T(8,128)(2,1)}, bf16[256,3072]{1,0:T(8,128)(2,1)}, u32[]{:S(2)}, u32[]{:S(2)}) collective-permute-start(bf16[256,3072]{1,0:T(8,128)(2,1)} %collective-permute-done.6), channel_id=1, source_target_pairs={{0,4},{1,5},{2,6},{3,7},{4,0},{5,1},{6,2},{7,3},{8,12},{9,13},{10,... | collective-permute-start | bytes 4718600 | tf_op jit(solution)/shard_map/ppermute | solution.py:455
  127.7 72.7 %collective-permute-start.9 = (bf16[288,3072]{1,0:T(8,128)(2,1)S(1)}, bf16[288,3072]{1,0:T(8,128)(2,1)}, u32[]{:S(2)}, u32[]{:S(2)}) collective-permute-start(bf16[288,3072]{1,0:T(8,128)(2,1)S(1)} %get-tuple-element.62), channel_id=1, source_target_pairs={{0,1},{1,0},{2,3},{3,2},{4,5},{5,4},{6,7},{7,6},{8,9},{9,8},{10,11... | collective-permute-start | bytes 5308424 | tf_op jit(solution)/shard_map/ppermute | solution.py:455
  129.2 76.2 %collective-permute-start.11 = (bf16[288,3072]{1,0:T(8,128)(2,1)}, bf16[288,3072]{1,0:T(8,128)(2,1)}, u32[]{:S(2)}, u32[]{:S(2)}) collective-permute-start(bf16[288,3072]{1,0:T(8,128)(2,1)} %collective-permute-done.10), channel_id=1, source_target_pairs={{0,1},{1,0},{2,3},{3,2},{4,5},{5,4},{6,7},{7,6},{8,9},{9,8},{10,11... | collective-permute-start | bytes 5308424 | tf_op jit(solution)/shard_map/ppermute | solution.py:455
  245.7 32.6 %copy-start.13 = (bf16[544,512]{1,0:T(8,128)(2,1)S(1)}, bf16[544,512]{1,0:T(8,128)(2,1)}, u32[]{:S(2)}) copy-start(bf16[544,512]{1,0:T(8,128)(2,1)} %get-tuple-element.90) | copy-start | bytes 1671172
  275.3 49.7 %collective-permute-start.18 = (bf16[544,512]{1,0:T(8,128)(2,1)}, bf16[544,512]{1,0:T(8,128)(2,1)S(1)}, u32[]{:S(2)}, u32[]{:S(2)}) collective-permute-start(bf16[544,512]{1,0:T(8,128)(2,1)} %get-tuple-element.95), channel_id=1, source_target_pairs={{0,1},{1,0},{2,3},{3,2},{4,5},{5,4},{6,7},{7,6},{8,9},{9,8},{10,11... | collective-permute-start | bytes 1671176 | tf_op jit(solution)/shard_map/ppermute | solution.py:455
  276.9 50.0 %collective-permute-start.16 = (bf16[544,512]{1,0:T(8,128)(2,1)}, bf16[544,512]{1,0:T(8,128)(2,1)S(1)}, u32[]{:S(2)}, u32[]{:S(2)}) collective-permute-start(bf16[544,512]{1,0:T(8,128)(2,1)} %get-tuple-element.89), channel_id=1, source_target_pairs={{0,4},{1,5},{2,6},{3,7},{4,0},{5,1},{6,2},{7,3},{8,12},{9,13},{10,... | collective-permute-start | bytes 1671176 | tf_op jit(solution)/shard_map/ppermute | solution.py:455
  278.3 48.5 %collective-permute-start.17 = (bf16[544,512]{1,0:T(8,128)(2,1)S(1)}, bf16[544,512]{1,0:T(8,128)(2,1)S(1)}, u32[]{:S(2)}, u32[]{:S(2)}) collective-permute-start(bf16[544,512]{1,0:T(8,128)(2,1)S(1)} %copy-done.13), channel_id=1, source_target_pairs={{0,5},{1,4},{2,7},{3,6},{4,1},{5,0},{6,3},{7,2},{8,13},{9,12},{10,... | collective-permute-start | bytes 1671176 | tf_op jit(solution)/shard_map/ppermute | solution.py:455
  304.7 20.3 %copy-start.14 = (bf16[544,256]{1,0:T(8,128)(2,1)S(1)}, bf16[544,256]{1,0:T(8,128)(2,1)}, u32[]{:S(2)}) copy-start(bf16[544,256]{1,0:T(8,128)(2,1)} %get-tuple-element.80) | copy-start | bytes 835588
  322.0 9.8 %collective-permute-start.15 = (bf16[544,256]{1,0:T(8,128)(2,1)}, bf16[544,256]{1,0:T(8,128)(2,1)S(1)}, u32[]{:S(2)}, u32[]{:S(2)}) collective-permute-start(bf16[544,256]{1,0:T(8,128)(2,1)} %get-tuple-element.85), channel_id=1, source_target_pairs={{0,1},{1,0},{2,3},{3,2},{4,5},{5,4},{6,7},{7,6},{8,9},{9,8},{10,11... | collective-permute-start | bytes 835592 | tf_op jit(solution)/shard_map/ppermute | solution.py:455
  323.6 14.7 %collective-permute-start.13 = (bf16[544,256]{1,0:T(8,128)(2,1)}, bf16[544,256]{1,0:T(8,128)(2,1)S(1)}, u32[]{:S(2)}, u32[]{:S(2)}) collective-permute-start(bf16[544,256]{1,0:T(8,128)(2,1)} %get-tuple-element.79), channel_id=1, source_target_pairs={{0,4},{1,5},{2,6},{3,7},{4,0},{5,1},{6,2},{7,3},{8,12},{9,13},{10,... | collective-permute-start | bytes 835592 | tf_op jit(solution)/shard_map/ppermute | solution.py:455
  325.0 1.8 copy-start.6
  325.0 13.2 %collective-permute-start.14 = (bf16[544,256]{1,0:T(8,128)(2,1)S(1)}, bf16[544,256]{1,0:T(8,128)(2,1)S(1)}, u32[]{:S(2)}, u32[]{:S(2)}) collective-permute-start(bf16[544,256]{1,0:T(8,128)(2,1)S(1)} %copy-done.14), channel_id=1, source_target_pairs={{0,5},{1,4},{2,7},{3,6},{4,1},{5,0},{6,3},{7,2},{8,13},{9,12},{10,... | collective-permute-start | bytes 835592 | tf_op jit(solution)/shard_map/ppermute | solution.py:455
  331.8 6.5 %copy-start.9 = (bf16[544,256]{1,0:T(8,128)(2,1)}, bf16[544,256]{1,0:T(8,128)(2,1)S(1)}, u32[]{:S(2)}) copy-start(bf16[544,256]{1,0:T(8,128)(2,1)S(1)} %collective-permute-done.15.rest_3_) | copy-start | bytes 835588
  (5 other events, 4.1 us)
Sparse Core Ops, SparseCore 0:
  11.1 73.9 all-gather.3
  87.3 128.2 all-gather.5
  217.7 69.4 all-gather.7

commit v2 on v1

--- a/solution.py
+++ b/solution.py
@@ -126,7 +126,7 @@
         scratch_shapes=[
             pltpu.SemaphoreType.DMA((6 * count * sum(heads for _, heads in groups),))
         ],
-        compiler_params=pltpu.CompilerParams(vmem_limit_bytes=32 * 1024 * 1024),
+        compiler_params=pltpu.CompilerParams(vmem_limit_bytes=58 * 1024 * 1024),
     )(columns, weights)
     return [outs[g * count : (g + 1) * count] for g in range(len(groups))]
 
@@ -289,9 +289,8 @@
         pltpu.make_async_copy(far.at[pl.ds(which[0] * rows, samples * rows)], near, sems.at[n])
         for n, (far, near, rows) in enumerate(((xt_far, xt, TXT), (xi_far, xi, IMG)))
     ]
-    for stream in range(2):
-        start(fetch(0, 0, stream))
-        tokens[stream].start()
+    start(fetch(0, 0, 0))
+    tokens[0].start()
     lead = lax.broadcasted_iota(jnp.int32, (KEYS, HD), 1) == 0
     for slot in range(slots):
         for i in range(items):
@@ -344,12 +343,17 @@
                 tops.at[n],
             )
 
-    for stream in range(2):
-        wait(fetch(0, 0, stream))
-        tokens[stream].wait()
-        if steps > 1:
+    wait(fetch(0, 0, 0))
+    tokens[0].wait()
+    start(fetch(0, 0, 1))
+    tokens[1].start()
+    project(0, 0)
+    wait(fetch(0, 0, 1))
+    tokens[1].wait()
+    if steps > 1:
+        for stream in range(2):
             start(fetch(1, 1, stream))
-        project(0, stream)
+    project(0, 1)
 
     def step(h, carry):
         for stream in range(2):
@@ -551,22 +555,26 @@
         if split > 1:
             weight = weight.reshape(outers, cores, len(hops), weight_rows, weight.shape[-1])
         received, columns = [], []
-        for flip in reversed(range(split)):
+        flips = list(range(split))
+        calls = [flips] if heads <= pair else [[flip] for flip in reversed(flips)]
+        for which in calls:
             parts = attend_group(
                 texts, images, weight, own_quarter, rows_from, tables, mask,
-                first, heads, (flip,), pair, apart,
+                first, heads, tuple(which), pair, apart,
             )
             weight, parts = lax.optimization_barrier((weight, parts))
             if not apart:
-                whole = parts[0]
+                whole = parts
                 parts = []
+                for part in whole:
+                    for k in range(ranks):
+                        text = part[k * text_rows : (k + 1) * text_rows]
+                        image = part[TXT + k * image_rows : TXT + (k + 1) * image_rows]
+                        parts.append(jnp.concatenate([text, image], axis=0))
+            for n, flip in enumerate(which):
                 for k in range(ranks):
-                    text = whole[k * text_rows : (k + 1) * text_rows]
-                    image = whole[TXT + k * image_rows : TXT + (k + 1) * image_rows]
-                    parts.append(jnp.concatenate([text, image], axis=0))
-            for k in range(ranks):
-                received.append(shift(parts[k], flip, ranks - k))
-                columns.append(head_owner(flip, k) * cols + first * HD)
+                    received.append(shift(parts[n * ranks + k], flip, ranks - k))
+                    columns.append(head_owner(flip, k) * cols + first * HD)
         return received, columns
 
     def place(received, columns, outs):

time: 354 us -> 347 us (0.980)
  local copies, waits for them, and re-layouts: 14.9 us -> 11 us
    pallas_call x2, Pallas kernels: 3.08 us -> 7.49 us  [cut_pieces(): pl.pallas_call(functools.partial(cut_kernel, groups, count, pair), in_spe...]
    pallas_call x4 -> x3, Pallas kernels: 93.7 us -> 89.7 us  [attend_group(): pl.pallas_call(body, in_specs=[in_hbm] * 2 + weight_specs + [in_vmem] * (...]
    unnamed x30 -> x26, local copies, waits for them, and re-layouts: 10.3 us -> 6.37 us
where the time goes in v2:
time: 347 us; the launch traced here: 342 us
  waiting for transfers between devices  161 us (46%)
  Pallas kernels  108 us (31%)
  starting transfers between devices  26.8 us (8%)
  other arithmetic  19.8 us (6%)
  between operations  15.8 us (5%)
  local copies, waits for them, and re-layouts  11 us (3%)
    ppermute x19, waiting for transfers between devices, permute(): return lax.ppermute(value, ('rep', 'seq'), pairs)  127 us
    pallas_call x3, Pallas kernels, attend_group(): pl.pallas_call(body, in_specs=[in_hbm] * 2 + weight_specs + [in_vmem] * (...  89.7 us
    all_gather x3, waiting for transfers between devices, gather(): lax.all_gather(block, 'rep', axis=0, tiled=True, axis_index_groups=gather...  33.3 us
    ppermute x19, starting transfers between devices, permute(): return lax.ppermute(value, ('rep', 'seq'), pairs)  26.7 us
    concatenate x2, other arithmetic, on_device(): jnp.concatenate(pieces, axis=0)  11.9 us
    pallas_call x2, Pallas kernels, cut_pieces(): pl.pallas_call(functools.partial(cut_kernel, groups, count, pair), in_spe...  7.49 us
  transfers between devices with their start and end apart: 22, of which 11 were waited for; matrix products, arithmetic and copies ran while one was open for 7% of the time, Pallas kernels for 30%

profile of v2, /device:TPU:0, one launch (start us, length us, event | category | flops | bytes accessed | tf_op | source)
XLA Modules:
  0.0 342.4 jit_solution(6581845878948051965)
XLA Ops:
  7.3 2.5 shard_map.105
  10.5 5.0 %shard_map.106 = (bf16[96,3072]{1,0:T(8,128)(2,1)}, bf16[96,3072]{1,0:T(8,128)(2,1)}, bf16[96,3072]{1,0:T(8,128)(2,1)}, bf16[96,1536]{1,0:T(8,128)(2,1)}, bf16[9...) custom-call(s32[3]{0:T(128)} %pad_add_fusion.2.columns, bf16[2,3,96,3072]{3,2,1,0:T(8,128)(2,1)} %bitcast.48), custom_call_target="tpu_custom_call" | custom-call | tf_op jit(solution)/shard_map/pallas_call | solution.py:114
  15.5 3.0 collective-permute-start.3
  18.5 2.0 collective-permute-start.1
  21.9 1.5 collective-permute-start.4
  23.5 3.0 collective-permute-done.3.rest_0_
  26.5 3.0 collective-permute-start.5
  32.9 2.5 shard_map.104
  36.6 22.2 %collective-permute-done.4.rest_1_ = bf16[96,1536]{1,0:T(8,128)(2,1)S(1)} collective-permute-done((bf16[96,1536]{1,0:T(8,128)(2,1)}, bf16[96,1536]{1,0:T(8,128)(2,1)S(1)}, u32[]{:S(2)}, u32[]{:S(2)}) %collective-permute-start.4) | collective-permute-done | bytes 294944 | tf_op jit(solution)/shard_map/ppermute | solution.py:459
  58.8 1.5 shard_map.108
  60.4 1.9 shard_map.107
  62.2 22.3 %all-gather.4.cloned.1.call-done = bf16[768,4608]{1,0:T(8,128)(2,1)} async-done(((bf16[96,4608]{1,0:T(8,128)(2,1)}), bf16[768,4608]{1,0:T(8,128)(2,1)}) %all-gather.4.cloned.1.call-update) | async-done | bytes 7077904 | tf_op jit(solution)/shard_map/all_gather | solution.py:503
  84.6 1.5 collective-permute-start.6
  92.2 29.2 %collective-permute-done.6 = bf16[256,3072]{1,0:T(8,128)(2,1)} collective-permute-done((bf16[256,3072]{1,0:T(8,128)(2,1)S(1)}, bf16[256,3072]{1,0:T(8,128)(2,1)}, u32[]{:S(2)}, u32[]{:S(2)}) %collective-permute-start.6) | collective-permute-done | bytes 1572896 | tf_op jit(solution)/shard_map/ppermute | solution.py:459
  122.8 1.9 constant_dynamic-slice_fusion.1
  125.4 1.8 fusion
  129.3 1.7 fusion.2
  133.0 28.5 %collective-permute-done.7 = bf16[256,3072]{1,0:T(8,128)(2,1)} collective-permute-done((bf16[256,3072]{1,0:T(8,128)(2,1)S(1)}, bf16[256,3072]{1,0:T(8,128)(2,1)}, u32[]{:S(2)}, u32[]{:S(2)}) %collective-permute-start.7) | collective-permute-done | bytes 1572896 | tf_op jit(solution)/shard_map/ppermute | solution.py:459
  161.5 32.7 %collective-permute-done.8 = bf16[256,3072]{1,0:T(8,128)(2,1)} collective-permute-done((bf16[256,3072]{1,0:T(8,128)(2,1)}, bf16[256,3072]{1,0:T(8,128)(2,1)}, u32[]{:S(2)}, u32[]{:S(2)}) %collective-permute-start.8) | collective-permute-done | bytes 1572896 | tf_op jit(solution)/shard_map/ppermute | solution.py:459
  194.2 5.7 %pad_maximum_fusion.1.xt = bf16[1024,3072]{1,0:T(8,128)(2,1)} fusion(bf16[256,3072]{1,0:T(8,128)(2,1)} %collective-permute-done.8, bf16[256,3072]{1,0:T(8,128)(2,1)} %collective-permute-done.7, bf16[256,3072]{1,0:T(8,128)(2,1)} %collective-permute-done.6, bf16[256,3072]{1,0:T(8,128)(2,1)S(1)} %copy-done.3), kind=kLoop, calls=%fused_computation.1 | loop fusion | flops 25165824 | bytes 12582912 | tf_op jit(solution)/shard_map/concatenate | solution.py:520
  199.9 5.0 %collective-permute-done.11 = bf16[288,3072]{1,0:T(8,128)(2,1)} collective-permute-done((bf16[288,3072]{1,0:T(8,128)(2,1)}, bf16[288,3072]{1,0:T(8,128)(2,1)}, u32[]{:S(2)}, u32[]{:S(2)}) %collective-permute-start.11) | collective-permute-done | bytes 1769504 | tf_op jit(solution)/shard_map/ppermute | solution.py:459
  204.9 6.1 %pad_maximum_fusion.xi = bf16[1152,3072]{1,0:T(8,128)(2,1)} fusion(bf16[288,3072]{1,0:T(8,128)(2,1)} %collective-permute-done.11, bf16[288,3072]{1,0:T(8,128)(2,1)} %collective-permute-done.10, bf16[288,3072]{1,0:T(8,128)(2,1)} %collective-permute-done.9, bf16[288,3072]{1,0:T(8,128)(2,1)S(1)} %get-tuple-element.61), kind=kLoop, calls=%fused_computation | loop fusion | flops 28311552 | bytes 14155776 | tf_op jit(solution)/shard_map/concatenate | solution.py:520
  211.0 4.0 %all-gather.6.cloned.1.call-done = bf16[2304,3072]{1,0:T(8,128)(2,1)} async-done(((bf16[288,3072]{1,0:T(8,128)(2,1)}), bf16[2304,3072]{1,0:T(8,128)(2,1)}) %all-gather.6.cloned.1.call-update) | async-done | bytes 14155792 | tf_op jit(solution)/shard_map/all_gather | solution.py:503
  215.8 30.2 %shard_map.110 = (bf16[544,512]{1,0:T(8,128)(2,1)}, bf16[544,512]{1,0:T(8,128)(2,1)}) custom-call(bf16[1024,3072]{1,0:T(8,128)(2,1)} %pad_maximum_fusion.1.xt, bf16[1152,3072]{1,0:T(8,128)(2,1)} %pad_maximum_fusion.xi, bf16[4,2,3,96,3072]{4,3,2,1,0:T(8,128)(2,1)} %bitcast.51, bf16[4,2,96,4608]{3,2,1,0:T(8,128)(2,1)} %bitcast.53, s32[4,2]{1,0:T(4,128)} %pad_add_fusion.places, ...), custom_call_target="tpu_custom_call" | custom-call | flops 15116271616 | bytes 25559040 | tf_op jit(solution)/shard_map/pallas_call | solution.py:401
  246.0 29.6 %shard_map.111 = (bf16[544,512]{1,0:T(8,128)(2,1)}, bf16[544,512]{1,0:T(8,128)(2,1)}) custom-call(bf16[1024,3072]{1,0:T(8,128)(2,1)} %pad_maximum_fusion.1.xt, bf16[1152,3072]{1,0:T(8,128)(2,1)} %pad_maximum_fusion.xi, bf16[4,2,3,96,3072]{4,3,2,1,0:T(8,128)(2,1)} %bitcast.52, bf16[4,2,96,4608]{3,2,1,0:T(8,128)(2,1)} %bitcast.54, s32[4,2]{1,0:T(4,128)} %pad_add_fusion.places, ...), custom_call_target="tpu_custom_call" | custom-call | flops 15116271616 | bytes 25559040 | tf_op jit(solution)/shard_map/pallas_call | solution.py:401
  277.0 1.5 collective-permute-start.16
  279.2 7.0 %all-gather.8.cloned.1.call-done = bf16[2304,1536]{1,0:T(8,128)(2,1)} async-done(((bf16[288,1536]{1,0:T(8,128)(2,1)}), bf16[2304,1536]{1,0:T(8,128)(2,1)}) %all-gather.8.cloned.1.call-update) | async-done | bytes 7077904 | tf_op jit(solution)/shard_map/all_gather | solution.py:503
  286.2 29.8 %shard_map.109 = (bf16[544,256]{1,0:T(8,128)(2,1)}, bf16[544,256]{1,0:T(8,128)(2,1)}, bf16[544,256]{1,0:T(8,128)(2,1)}, bf16[544,256]{1,0:T(8,128)(2,1)}) custom-call(bf16[1024,3072]{1,0:T(8,128)(2,1)} %pad_maximum_fusion.1.xt, bf16[1152,3072]{1,0:T(8,128)(2,1)} %pad_maximum_fusion.xi, bf16[4,2,3,96,1536]{4,3,2,1,0:T(8,128)(2,1)} %bitcast.56, ...), custom_call_target="tpu_custom_call" | custom-call | flops 15116271616 | bytes 22806528 | tf_op jit(solution)/shard_map/pallas_call | solution.py:401
  316.0 1.5 collective-permute-start.13
  322.5 3.0 shard_map.112
  325.8 6.5 %collective-permute-done.14.rest_2_ = bf16[544,256]{1,0:T(8,128)(2,1)S(1)} collective-permute-done((bf16[544,256]{1,0:T(8,128)(2,1)}, bf16[544,256]{1,0:T(8,128)(2,1)S(1)}, u32[]{:S(2)}, u32[]{:S(2)}) %collective-permute-start.14) | collective-permute-done | bytes 278560 | tf_op jit(solution)/shard_map/ppermute | solution.py:459
  333.1 2.3 shard_map.113
  (81 shorter events, 26.6 us)
Async XLA Ops:
  7.2 23.0 %copy-start = (bf16[1,288,3072]{2,1,0:T(8,128)(2,1)S(1)}, bf16[1,288,3072]{2,1,0:T(8,128)(2,1)}, u32[]{:S(2)}) copy-start(bf16[1,288,3072]{2,1,0:T(8,128)(2,1)} %param.10) | copy-start | bytes 5308420
  7.2 77.4 %all-gather.4.cloned.1.call-start = ((), (), s32[]{:S(2)}) async-start(), calls=%async_computation | async-start | bytes 7962624 | tf_op jit(solution)/shard_map/all_gather | solution.py:503
  10.4 204.6 %all-gather.6.cloned.1.call-start = ((), (), s32[]{:S(2)}) async-start(), calls=%async_computation.1 | async-start | bytes 15925248 | tf_op jit(solution)/shard_map/all_gather | solution.py:503
  15.4 72.8 %copy-start.11 = (f32[2,2,128]{2,1,0:T(2,128)S(1)}, f32[2,2,128]{2,1,0:T(2,128)}, u32[]{:S(2)}) copy-start(f32[2,2,128]{2,1,0:T(2,128)} %param.12) | copy-start | bytes 6148
  15.5 11.1 %collective-permute-start.3 = (bf16[96,1536]{1,0:T(8,128)(2,1)}, bf16[96,1536]{1,0:T(8,128)(2,1)S(1)}, u32[]{:S(2)}, u32[]{:S(2)}) collective-permute-start(bf16[96,1536]{1,0:T(8,128)(2,1)} %get-tuple-element.56), channel_id=1, source_target_pairs={{0,1},{1,0},{2,3},{3,2},{4,5},{5,4},{6,7},{7,6},{8,9},{9,8},{10,11... | collective-permute-start | bytes 884744 | tf_op jit(solution)/shard_map/ppermute | solution.py:459
  18.5 41.9 %collective-permute-start = (bf16[96,3072]{1,0:T(8,128)(2,1)}, bf16[96,3072]{1,0:T(8,128)(2,1)S(1)}, u32[]{:S(2)}, u32[]{:S(2)}) collective-permute-start(bf16[96,3072]{1,0:T(8,128)(2,1)} %get-tuple-element.53), channel_id=1, source_target_pairs={{0,1},{1,0},{2,3},{3,2},{4,5},{5,4},{6,7},{7,6},{8,9},{9,8},{10,11... | collective-permute-start | bytes 1769480 | tf_op jit(solution)/shard_map/ppermute | solution.py:459
  18.5 41.8 %collective-permute-start.1 = (bf16[96,3072]{1,0:T(8,128)(2,1)}, bf16[96,3072]{1,0:T(8,128)(2,1)S(1)}, u32[]{:S(2)}, u32[]{:S(2)}) collective-permute-start(bf16[96,3072]{1,0:T(8,128)(2,1)} %get-tuple-element.54), channel_id=1, source_target_pairs={{0,4},{1,5},{2,6},{3,7},{4,0},{5,1},{6,2},{7,3},{8,12},{9,13},{10,... | collective-permute-start | bytes 1769480 | tf_op jit(solution)/shard_map/ppermute | solution.py:459
  20.5 39.8 %collective-permute-start.2 = (bf16[96,3072]{1,0:T(8,128)(2,1)}, bf16[96,3072]{1,0:T(8,128)(2,1)S(1)}, u32[]{:S(2)}, u32[]{:S(2)}) collective-permute-start(bf16[96,3072]{1,0:T(8,128)(2,1)} %get-tuple-element.55), channel_id=1, source_target_pairs={{0,5},{1,4},{2,7},{3,6},{4,1},{5,0},{6,3},{7,2},{8,13},{9,12},{10,... | collective-permute-start | bytes 1769480 | tf_op jit(solution)/shard_map/ppermute | solution.py:459
  21.9 36.9 %collective-permute-start.4 = (bf16[96,1536]{1,0:T(8,128)(2,1)}, bf16[96,1536]{1,0:T(8,128)(2,1)S(1)}, u32[]{:S(2)}, u32[]{:S(2)}) collective-permute-start(bf16[96,1536]{1,0:T(8,128)(2,1)} %get-tuple-element.57), channel_id=1, source_target_pairs={{0,4},{1,5},{2,6},{3,7},{4,0},{5,1},{6,2},{7,3},{8,12},{9,13},{10,... | collective-permute-start | bytes 884744 | tf_op jit(solution)/shard_map/ppermute | solution.py:459
  26.5 32.3 %collective-permute-start.5 = (bf16[96,1536]{1,0:T(8,128)(2,1)}, bf16[96,1536]{1,0:T(8,128)(2,1)S(1)}, u32[]{:S(2)}, u32[]{:S(2)}) collective-permute-start(bf16[96,1536]{1,0:T(8,128)(2,1)} %get-tuple-element.58), channel_id=1, source_target_pairs={{0,5},{1,4},{2,7},{3,6},{4,1},{5,0},{6,3},{7,2},{8,13},{9,12},{10,... | collective-permute-start | bytes 884744 | tf_op jit(solution)/shard_map/ppermute | solution.py:459
  30.2 1.4 copy-start.1
  31.6 1.4 copy-start.4
  35.4 1.1 copy-start.2
  58.8 25.8 %copy-start.3 = (bf16[256,3072]{1,0:T(8,128)(2,1)S(1)}, bf16[256,3072]{1,0:T(8,128)(2,1)}, u32[]{:S(2)}) copy-start(bf16[256,3072]{1,0:T(8,128)(2,1)} %copy-done.2) | copy-start | bytes 4718596
  84.6 201.6 %all-gather.8.cloned.1.call-start = ((), (), s32[]{:S(2)}) async-start(), calls=%async_computation.2 | async-start | bytes 7962624 | tf_op jit(solution)/shard_map/all_gather | solution.py:503
  84.6 36.7 %collective-permute-start.6 = (bf16[256,3072]{1,0:T(8,128)(2,1)S(1)}, bf16[256,3072]{1,0:T(8,128)(2,1)}, u32[]{:S(2)}, u32[]{:S(2)}) collective-permute-start(bf16[256,3072]{1,0:T(8,128)(2,1)S(1)} %copy-done.3), channel_id=1, source_target_pairs={{0,1},{1,0},{2,3},{3,2},{4,5},{5,4},{6,7},{7,6},{8,9},{9,8},{10,11... | collective-permute-start | bytes 4718600 | tf_op jit(solution)/shard_map/ppermute | solution.py:459
  86.2 42.5 %collective-permute-start.10 = (bf16[288,3072]{1,0:T(8,128)(2,1)S(1)}, bf16[288,3072]{1,0:T(8,128)(2,1)}, u32[]{:S(2)}, u32[]{:S(2)}) collective-permute-start(bf16[288,3072]{1,0:T(8,128)(2,1)S(1)} %get-tuple-element.61), channel_id=1, source_target_pairs={{0,4},{1,5},{2,6},{3,7},{4,0},{5,1},{6,2},{7,3},{8,12},{9,13},{10,... | collective-permute-start | bytes 5308424 | tf_op jit(solution)/shard_map/ppermute | solution.py:459
  87.6 43.5 %collective-permute-start.12 = (s32[1]{0:T(128)}, s32[1]{0:T(128)}, u32[]{:S(2)}, u32[]{:S(2)}) collective-permute-start(s32[1]{0:T(128)} %param.14), channel_id=1, source_target_pairs={{0,4},{1,5},{2,6},{3,7},{4,0},{5,1},{6,2},{7,3},{8,12},{9,13},{10,... | collective-permute-start | bytes 20 | tf_op jit(solution)/shard_map/ppermute | solution.py:459
  90.7 70.8 %collective-permute-start.7 = (bf16[256,3072]{1,0:T(8,128)(2,1)S(1)}, bf16[256,3072]{1,0:T(8,128)(2,1)}, u32[]{:S(2)}, u32[]{:S(2)}) collective-permute-start(bf16[256,3072]{1,0:T(8,128)(2,1)S(1)} %copy-done.3), channel_id=1, source_target_pairs={{0,4},{1,5},{2,6},{3,7},{4,0},{5,1},{6,2},{7,3},{8,12},{9,13},{10,... | collective-permute-start | bytes 4718600 | tf_op jit(solution)/shard_map/ppermute | solution.py:459
  121.3 72.8 %collective-permute-start.8 = (bf16[256,3072]{1,0:T(8,128)(2,1)}, bf16[256,3072]{1,0:T(8,128)(2,1)}, u32[]{:S(2)}, u32[]{:S(2)}) collective-permute-start(bf16[256,3072]{1,0:T(8,128)(2,1)} %collective-permute-done.6), channel_id=1, source_target_pairs={{0,4},{1,5},{2,6},{3,7},{4,0},{5,1},{6,2},{7,3},{8,12},{9,13},{10,... | collective-permute-start | bytes 4718600 | tf_op jit(solution)/shard_map/ppermute | solution.py:459
  127.2 72.7 %collective-permute-start.9 = (bf16[288,3072]{1,0:T(8,128)(2,1)S(1)}, bf16[288,3072]{1,0:T(8,128)(2,1)}, u32[]{:S(2)}, u32[]{:S(2)}) collective-permute-start(bf16[288,3072]{1,0:T(8,128)(2,1)S(1)} %get-tuple-element.61), channel_id=1, source_target_pairs={{0,1},{1,0},{2,3},{3,2},{4,5},{5,4},{6,7},{7,6},{8,9},{9,8},{10,11... | collective-permute-start | bytes 5308424 | tf_op jit(solution)/shard_map/ppermute | solution.py:459
  128.7 76.2 %collective-permute-start.11 = (bf16[288,3072]{1,0:T(8,128)(2,1)}, bf16[288,3072]{1,0:T(8,128)(2,1)}, u32[]{:S(2)}, u32[]{:S(2)}) collective-permute-start(bf16[288,3072]{1,0:T(8,128)(2,1)} %collective-permute-done.10), channel_id=1, source_target_pairs={{0,1},{1,0},{2,3},{3,2},{4,5},{5,4},{6,7},{7,6},{8,9},{9,8},{10,11... | collective-permute-start | bytes 5308424 | tf_op jit(solution)/shard_map/ppermute | solution.py:459
  246.0 32.5 %copy-start.12 = (bf16[544,512]{1,0:T(8,128)(2,1)S(1)}, bf16[544,512]{1,0:T(8,128)(2,1)}, u32[]{:S(2)}) copy-start(bf16[544,512]{1,0:T(8,128)(2,1)} %get-tuple-element.88) | copy-start | bytes 1671172
  275.6 43.4 %collective-permute-start.18 = (bf16[544,512]{1,0:T(8,128)(2,1)}, bf16[544,512]{1,0:T(8,128)(2,1)S(1)}, u32[]{:S(2)}, u32[]{:S(2)}) collective-permute-start(bf16[544,512]{1,0:T(8,128)(2,1)} %get-tuple-element.93), channel_id=1, source_target_pairs={{0,1},{1,0},{2,3},{3,2},{4,5},{5,4},{6,7},{7,6},{8,9},{9,8},{10,11... | collective-permute-start | bytes 1671176 | tf_op jit(solution)/shard_map/ppermute | solution.py:459
  277.0 43.9 %collective-permute-start.16 = (bf16[544,512]{1,0:T(8,128)(2,1)}, bf16[544,512]{1,0:T(8,128)(2,1)S(1)}, u32[]{:S(2)}, u32[]{:S(2)}) collective-permute-start(bf16[544,512]{1,0:T(8,128)(2,1)} %get-tuple-element.87), channel_id=1, source_target_pairs={{0,4},{1,5},{2,6},{3,7},{4,0},{5,1},{6,2},{7,3},{8,12},{9,13},{10,... | collective-permute-start | bytes 1671176 | tf_op jit(solution)/shard_map/ppermute | solution.py:459
  278.5 42.4 %collective-permute-start.17 = (bf16[544,512]{1,0:T(8,128)(2,1)S(1)}, bf16[544,512]{1,0:T(8,128)(2,1)S(1)}, u32[]{:S(2)}, u32[]{:S(2)}) collective-permute-start(bf16[544,512]{1,0:T(8,128)(2,1)S(1)} %copy-done.12), channel_id=1, source_target_pairs={{0,5},{1,4},{2,7},{3,6},{4,1},{5,0},{6,3},{7,2},{8,13},{9,12},{10,... | collective-permute-start | bytes 1671176 | tf_op jit(solution)/shard_map/ppermute | solution.py:459
  316.0 9.8 %collective-permute-start.13 = (bf16[544,256]{1,0:T(8,128)(2,1)}, bf16[544,256]{1,0:T(8,128)(2,1)S(1)}, u32[]{:S(2)}, u32[]{:S(2)}) collective-permute-start(bf16[544,256]{1,0:T(8,128)(2,1)} %get-tuple-element.81), channel_id=1, source_target_pairs={{0,1},{1,0},{2,3},{3,2},{4,5},{5,4},{6,7},{7,6},{8,9},{9,8},{10,11... | collective-permute-start | bytes 835592 | tf_op jit(solution)/shard_map/ppermute | solution.py:459
  317.6 14.7 %collective-permute-start.14 = (bf16[544,256]{1,0:T(8,128)(2,1)}, bf16[544,256]{1,0:T(8,128)(2,1)S(1)}, u32[]{:S(2)}, u32[]{:S(2)}) collective-permute-start(bf16[544,256]{1,0:T(8,128)(2,1)} %get-tuple-element.82), channel_id=1, source_target_pairs={{0,4},{1,5},{2,6},{3,7},{4,0},{5,1},{6,2},{7,3},{8,12},{9,13},{10,... | collective-permute-start | bytes 835592 | tf_op jit(solution)/shard_map/ppermute | solution.py:459
  319.0 1.8 copy-start.5
  319.0 13.2 %collective-permute-start.15 = (bf16[544,256]{1,0:T(8,128)(2,1)}, bf16[544,256]{1,0:T(8,128)(2,1)S(1)}, u32[]{:S(2)}, u32[]{:S(2)}) collective-permute-start(bf16[544,256]{1,0:T(8,128)(2,1)} %get-tuple-element.83), channel_id=1, source_target_pairs={{0,5},{1,4},{2,7},{3,6},{4,1},{5,0},{6,3},{7,2},{8,13},{9,12},{10,... | collective-permute-start | bytes 835592 | tf_op jit(solution)/shard_map/ppermute | solution.py:459
  325.8 6.5 %copy-start.8 = (bf16[544,256]{1,0:T(8,128)(2,1)}, bf16[544,256]{1,0:T(8,128)(2,1)S(1)}, u32[]{:S(2)}) copy-start(bf16[544,256]{1,0:T(8,128)(2,1)S(1)} %collective-permute-done.13.rest_1_) | copy-start | bytes 835588
  332.3 0.8 copy-start.10
  (3 other events, 2.3 us)
Sparse Core Ops, SparseCore 0:
  10.6 73.9 all-gather.3
  86.8 128.2 all-gather.5
  216.7 69.4 all-gather.7
